TPU v7x, 32 devices: a whole 2x2x4 slice. The times are simulated.
32 devices in a mesh: clip: 8 (over z, y), unit: 4 (over x, core).
Axes of the slice: x: 2, y: 2, z: 4, core: 2. Of those that a mesh axis runs over, the one named last changes fastest.
Arguments:
- tokens: bfloat16 [16, 392, 16, 192], P('clip', 'unit'), may hold values from -6 to 6
- first_gain: bfloat16 [192], replicated, may hold values from 0.5 to 1.5
- first_shift: bfloat16 [192], replicated, may hold values from -1 to 1
- proj_weight: bfloat16 [192, 384], replicated, may hold values from -0.875 to 0.875
- proj_bias: bfloat16 [384], replicated, may hold values from -1 to 1
- qkv_weight: bfloat16 [192, 1152], replicated, may hold values from -0.625 to 0.625
- query_bias: bfloat16 [384], replicated, may hold values from -1.5 to 1.5
- value_bias: bfloat16 [384], replicated, may hold values from -1.5 to 1.5
- output_weight: bfloat16 [384, 384], replicated, may hold values from -3.5 to 3.5
- output_bias: bfloat16 [384], replicated, may hold values from -1 to 1
- second_gain: bfloat16 [384], replicated, may hold values from 0.5 to 1.5
- second_shift: bfloat16 [384], replicated, may hold values from -1 to 1
- expand_weight: bfloat16 [384, 1536], replicated, may hold values from -0.3125 to 0.3125
- expand_bias: bfloat16 [1536], replicated, may hold values from -1.5 to 1.5
- shrink_weight: bfloat16 [1536, 384], replicated, may hold values from -0.21875 to 0.21875
- shrink_bias: bfloat16 [384], replicated, may hold values from -1 to 1
- frame_counts: int32 [16], P('clip'), may hold values from 1 to 8, as said below
- unit_frames: int32 [16, 392], P('clip', 'unit'), may hold values from 0 to 7, as said below
- cotangent: bfloat16 [16, 392, 4, 384], P('clip', 'unit'), may hold values from -6 to 6
Outputs:
- layer_out: float32 [16, 392, 4, 384], P('clip', 'unit')
- input_grad: float32 [16, 392, 16, 192], P('clip', 'unit')
- first_gain_grad: float32 [192], P('unit')
- first_shift_grad: float32 [192], P('unit')
- proj_weight_grad: float32 [192, 384], P(None, 'unit')
- proj_bias_grad: float32 [384], P('unit')
- qkv_weight_grad: float32 [192, 1152], P(None, 'unit')
- query_bias_grad: float32 [384], P('unit')
- value_bias_grad: float32 [384], P('unit')
- output_weight_grad: float32 [384, 384], P(None, 'unit')
- output_bias_grad: float32 [384], P('unit')
- second_gain_grad: float32 [384], P('unit')
- second_shift_grad: float32 [384], P('unit')
- expand_weight_grad: float32 [384, 1536], P(None, 'unit')
- expand_bias_grad: float32 [1536], P('unit')
- shrink_weight_grad: float32 [1536, 384], P('unit')
- shrink_bias_grad: float32 [384], P('unit')
Inputs may be any that keep to these rules, and one draw needn't show every extreme that they name: `frame_counts`: each clip's count of valid frames; some clip has all 8. `unit_frames`: each frame of a clip has exactly 49 units, and every device along unit holds at least one unit of every frame of each of its clips.
All inputs are finite; a program needn't handle non-finite values.
Results may differ from a plain program's by a relative error of at most 0.012.
Values may be sent and summed in bfloat16 or wider, within the bound.
No kernel may reach another device: no remote copies, remote signals or barrier semaphores. Data moves between devices by JAX's collectives and lax.ppermute only.
A program may use at most 384 MiB of HBM per device.

v0:
```python
import jax
import jax.numpy as jnp
from jax import lax
from jax.sharding import PartitionSpec as P

D_IN = 192
D_OUT = 384
HEADS = 4
HEAD_DIM = 96


def layer_norm(values, gain_vector, shift_vector):
    center = values - jnp.mean(values, axis=-1, keepdims=True)
    spread = jnp.mean(center * center, axis=-1, keepdims=True)
    return center * lax.rsqrt(spread + 1e-06) * gain_vector + shift_vector


def pool_units(tensor):
    leading = tensor.shape[:-2]
    channels = tensor.shape[-1]
    blocks = tensor.reshape(leading + (2, 2, 2, 2, channels))
    return jnp.mean(blocks, axis=(-4, -2)).reshape(leading + (4, channels))


def spread_units(tensor):
    leading = tensor.shape[:-2]
    channels = tensor.shape[-1]
    blocks = tensor.reshape(leading + (2, 1, 2, 1, channels))
    widened = jnp.broadcast_to(blocks, leading + (2, 2, 2, 2, channels)) * 0.25
    return widened.reshape(leading + (16, channels))


def gelu_exact(values):
    return jax.nn.gelu(values, approximate=False)


def shards(
    tokens,
    first_gain,
    first_shift,
    proj_weight,
    proj_bias,
    qkv_weight,
    query_bias,
    value_bias,
    output_weight,
    output_bias,
    second_gain,
    second_shift,
    expand_weight,
    expand_bias,
    shrink_weight,
    shrink_bias,
    frame_counts,
    unit_frames,
    cotangent,
):
    clip_count = tokens.shape[0]
    unit_count = tokens.shape[1]
    own_rows = unit_count * 16
    score_scale = HEAD_DIM ** (-0.5)
    inputs = tokens.astype(jnp.float32).reshape(-1, D_IN)
    normed_full, first_pull = jax.vjp(
        layer_norm, inputs, first_gain.astype(jnp.float32), first_shift.astype(jnp.float32)
    )
    normed = normed_full.astype(jnp.bfloat16)
    projection = jnp.dot(
        normed, proj_weight, preferred_element_type=jnp.float32
    ) + proj_bias.astype(jnp.float32)
    residual = pool_units(projection.reshape(clip_count, unit_count, 16, D_OUT)).reshape(-1, D_OUT)
    projected = jnp.dot(normed, qkv_weight, preferred_element_type=jnp.float32)
    projected = projected.reshape(clip_count, unit_count, 16, 3 * D_OUT)
    query_part = projected[..., :D_OUT]
    own_keys = (
        projected[..., D_OUT : 2 * D_OUT].astype(jnp.bfloat16).reshape(clip_count, own_rows, D_OUT)
    )
    own_values = (projected[..., 2 * D_OUT :] + value_bias.astype(jnp.float32)).astype(jnp.bfloat16)
    own_values = own_values.reshape(clip_count, own_rows, D_OUT)
    key_rows, value_rows, frame_rows = (
        lax.all_gather(own_keys, "unit", axis=1, tiled=True),
        lax.all_gather(own_values, "unit", axis=1, tiled=True),
        lax.all_gather(unit_frames, "unit", axis=1, tiled=True),
    )
    queries = (pool_units(query_part) + query_bias.astype(jnp.float32)).astype(jnp.bfloat16)
    query_heads = queries.reshape(clip_count, unit_count * 4, HEADS, HEAD_DIM)
    key_valid = jnp.repeat(frame_rows < frame_counts[:, None], 16, axis=1)

    def clip_scores(query_one, key_one, valid_one):
        key_heads = key_one.reshape(-1, HEADS, HEAD_DIM)
        scores = (
            jnp.einsum("qhd,khd->hqk", query_one, key_heads, preferred_element_type=jnp.float32)
            * score_scale
        )
        return jnp.where(valid_one[None, None, :], scores, -1e30)

    def attend(operands):
        query_one, key_one, value_one, valid_one = operands
        scores = clip_scores(query_one, key_one, valid_one)
        highest = jnp.max(scores, axis=-1, keepdims=True)
        weights = jnp.exp(scores - highest)
        denominator = jnp.sum(weights, axis=-1, keepdims=True)
        probability = (weights / denominator).astype(jnp.bfloat16)
        attended_one = jnp.einsum(
            "hqk,khd->qhd",
            probability,
            value_one.reshape(-1, HEADS, HEAD_DIM),
            preferred_element_type=jnp.float32,
        )
        return (attended_one.reshape(-1, D_OUT), highest + jnp.log(denominator))

    attended, log_total = lax.map(attend, (query_heads, key_rows, value_rows, key_valid))
    attended = attended.reshape(-1, D_OUT).astype(jnp.bfloat16)
    hidden = residual + jnp.dot(attended, output_weight, preferred_element_type=jnp.float32)
    hidden = hidden + output_bias.astype(jnp.float32)
    second_full, second_pull = jax.vjp(
        layer_norm, hidden, second_gain.astype(jnp.float32), second_shift.astype(jnp.float32)
    )
    second = second_full.astype(jnp.bfloat16)
    before = jnp.dot(
        second, expand_weight, preferred_element_type=jnp.float32
    ) + expand_bias.astype(jnp.float32)
    active_full, gelu_pull = jax.vjp(gelu_exact, before)
    active = active_full.astype(jnp.bfloat16)
    layer_out = hidden + jnp.dot(active, shrink_weight, preferred_element_type=jnp.float32)
    layer_out = layer_out + shrink_bias.astype(jnp.float32)
    upstream = cotangent.reshape(-1, D_OUT)
    upstream_full = upstream.astype(jnp.float32)
    shrink_bias_part = jnp.sum(upstream_full, axis=0)
    shrink_weight_part = jnp.dot(active.T, upstream, preferred_element_type=jnp.float32)
    active_grad = jnp.dot(upstream, shrink_weight.T, preferred_element_type=jnp.float32)
    before_grad = gelu_pull(active_grad)[0].astype(jnp.bfloat16)
    expand_bias_part = jnp.sum(before_grad.astype(jnp.float32), axis=0)
    expand_weight_part = jnp.dot(second.T, before_grad, preferred_element_type=jnp.float32)
    second_grad = jnp.dot(before_grad, expand_weight.T, preferred_element_type=jnp.float32)
    hidden_back, second_gain_part, second_shift_part = second_pull(second_grad)
    hidden_grad = (upstream_full + hidden_back).astype(jnp.bfloat16)
    output_bias_part = jnp.sum(hidden_grad.astype(jnp.float32), axis=0)
    output_weight_part = jnp.dot(attended.T, hidden_grad, preferred_element_type=jnp.float32)
    attended_grad = jnp.dot(
        hidden_grad, output_weight.T, preferred_element_type=jnp.float32
    ).astype(jnp.bfloat16)
    attended_heads = attended_grad.reshape(clip_count, unit_count * 4, HEADS, HEAD_DIM)

    def score_grads(query_one, key_one, value_one, valid_one, total_one, grad_one):
        scores = clip_scores(query_one, key_one, valid_one)
        probability = jnp.exp(scores - total_one)
        value_heads = value_one.reshape(-1, HEADS, HEAD_DIM)
        probs_grad = jnp.einsum(
            "qhd,khd->hqk", grad_one, value_heads, preferred_element_type=jnp.float32
        )
        return (probability, probs_grad)

    def attend_back(operands):
        query_one, key_one, value_one, valid_one, total_one, grad_one = operands
        probability, probs_grad = score_grads(
            query_one, key_one, value_one, valid_one, total_one, grad_one
        )
        row_inner = jnp.sum(probability * probs_grad, axis=-1, keepdims=True)
        score_grad = (probability * (probs_grad - row_inner)).astype(jnp.bfloat16)
        query_back = (
            jnp.einsum(
                "hqk,khd->qhd",
                score_grad,
                key_one.reshape(-1, HEADS, HEAD_DIM),
                preferred_element_type=jnp.float32,
            )
            * score_scale
        )
        key_back = (
            jnp.einsum("hqk,qhd->khd", score_grad, query_one, preferred_element_type=jnp.float32)
            * score_scale
        )
        value_back = jnp.einsum(
            "hqk,qhd->khd",
            probability.astype(jnp.bfloat16),
            grad_one,
            preferred_element_type=jnp.float32,
        )
        return (
            query_back.reshape(-1, D_OUT),
            key_back.reshape(-1, D_OUT),
            value_back.reshape(-1, D_OUT),
        )

    query_grad, key_grad_all, value_grad_all = lax.map(
        attend_back, (query_heads, key_rows, value_rows, key_valid, log_total, attended_heads)
    )
    key_grad, value_grad = (
        lax.psum_scatter(
            key_grad_all.astype(jnp.bfloat16), "unit", scatter_dimension=1, tiled=True
        ).astype(jnp.float32),
        lax.psum_scatter(
            value_grad_all.astype(jnp.bfloat16), "unit", scatter_dimension=1, tiled=True
        ).astype(jnp.float32),
    )
    query_grad = query_grad.reshape(clip_count, unit_count, 4, D_OUT)
    query_bias_part = jnp.sum(query_grad, axis=(0, 1, 2))
    value_bias_part = jnp.sum(value_grad, axis=(0, 1))
    projected_grad = jnp.concatenate(
        [
            spread_units(query_grad),
            key_grad.reshape(clip_count, unit_count, 16, D_OUT),
            value_grad.reshape(clip_count, unit_count, 16, D_OUT),
        ],
        axis=-1,
    )
    projected_grad = projected_grad.astype(jnp.bfloat16).reshape(-1, 3 * D_OUT)
    proj_grad = spread_units(
        hidden_grad.astype(jnp.float32).reshape(clip_count, unit_count, 4, D_OUT)
    )
    proj_grad = proj_grad.astype(jnp.bfloat16).reshape(-1, D_OUT)
    proj_bias_part = jnp.sum(proj_grad.astype(jnp.float32), axis=0)
    proj_weight_part = jnp.dot(normed.T, proj_grad, preferred_element_type=jnp.float32)
    qkv_weight_part = jnp.dot(normed.T, projected_grad, preferred_element_type=jnp.float32)
    normed_grad = jnp.dot(projected_grad, qkv_weight.T, preferred_element_type=jnp.float32)
    normed_grad = normed_grad + jnp.dot(
        proj_grad, proj_weight.T, preferred_element_type=jnp.float32
    )
    input_grad, first_gain_part, first_shift_part = first_pull(normed_grad)
    shares = (
        lax.psum_scatter(
            first_gain_part.astype(jnp.bfloat16), "unit", scatter_dimension=0, tiled=True
        ).astype(jnp.float32),
        lax.psum_scatter(
            first_shift_part.astype(jnp.bfloat16), "unit", scatter_dimension=0, tiled=True
        ).astype(jnp.float32),
        lax.psum_scatter(
            proj_weight_part.astype(jnp.bfloat16), "unit", scatter_dimension=1, tiled=True
        ).astype(jnp.float32),
        lax.psum_scatter(
            proj_bias_part.astype(jnp.bfloat16), "unit", scatter_dimension=0, tiled=True
        ).astype(jnp.float32),
        lax.psum_scatter(
            qkv_weight_part.astype(jnp.bfloat16), "unit", scatter_dimension=1, tiled=True
        ).astype(jnp.float32),
        lax.psum_scatter(
            query_bias_part.astype(jnp.bfloat16), "unit", scatter_dimension=0, tiled=True
        ).astype(jnp.float32),
        lax.psum_scatter(
            value_bias_part.astype(jnp.bfloat16), "unit", scatter_dimension=0, tiled=True
        ).astype(jnp.float32),
        lax.psum_scatter(
            output_weight_part.astype(jnp.bfloat16), "unit", scatter_dimension=1, tiled=True
        ).astype(jnp.float32),
        lax.psum_scatter(
            output_bias_part.astype(jnp.bfloat16), "unit", scatter_dimension=0, tiled=True
        ).astype(jnp.float32),
        lax.psum_scatter(
            second_gain_part.astype(jnp.bfloat16), "unit", scatter_dimension=0, tiled=True
        ).astype(jnp.float32),
        lax.psum_scatter(
            second_shift_part.astype(jnp.bfloat16), "unit", scatter_dimension=0, tiled=True
        ).astype(jnp.float32),
        lax.psum_scatter(
            expand_weight_part.astype(jnp.bfloat16), "unit", scatter_dimension=1, tiled=True
        ).astype(jnp.float32),
        lax.psum_scatter(
            expand_bias_part.astype(jnp.bfloat16), "unit", scatter_dimension=0, tiled=True
        ).astype(jnp.float32),
        lax.psum_scatter(
            shrink_weight_part.astype(jnp.bfloat16), "unit", scatter_dimension=0, tiled=True
        ).astype(jnp.float32),
        lax.psum_scatter(
            shrink_bias_part.astype(jnp.bfloat16), "unit", scatter_dimension=0, tiled=True
        ).astype(jnp.float32),
    )
    totals = lax.psum(
        (
            shares[0],
            shares[1],
            shares[2],
            shares[3],
            shares[4],
            shares[5],
            shares[6],
            shares[7],
            shares[8],
            shares[9],
            shares[10],
            shares[11],
            shares[12],
            shares[13],
            shares[14],
        ),
        "clip",
    )
    return (
        layer_out.reshape(clip_count, unit_count, 4, D_OUT),
        input_grad.reshape(tokens.shape),
        totals[0],
        totals[1],
        totals[2],
        totals[3],
        totals[4],
        totals[5],
        totals[6],
        totals[7],
        totals[8],
        totals[9],
        totals[10],
        totals[11],
        totals[12],
        totals[13],
        totals[14],
    )


def solution(mesh):
    placed = (
        P("clip", "unit", None, None),
        P(),
        P(),
        P(),
        P(),
        P(),
        P(),
        P(),
        P(),
        P(),
        P(),
        P(),
        P(),
        P(),
        P(),
        P(),
        P("clip"),
        P("clip", "unit"),
        P("clip", "unit", None, None),
    )
    return jax.shard_map(
        shards,
        mesh=mesh,
        in_specs=placed,
        out_specs=(
            P("clip", "unit", None, None),
            P("clip", "unit", None, None),
            P("unit"),
            P("unit"),
            P(None, "unit"),
            P("unit"),
            P(None, "unit"),
            P("unit"),
            P("unit"),
            P(None, "unit"),
            P("unit"),
            P("unit"),
            P("unit"),
            P(None, "unit"),
            P("unit"),
            P("unit", None),
            P("unit"),
        ),
        check_vma=False,
    )
```

profile of v0, /device:TPU:0, one launch (start us, length us, event | category | flops | bytes accessed | tf_op | source)
XLA Modules:
  0.0 959.8 jit_solution(1600567877140022703)
XLA Ops:
  27.8 10.8 %copy.91 = bf16[2,1568,384]{2,0,1:T(2,128)(2,1)} copy(bf16[2,1568,384]{2,1,0:T(8,128)(2,1)S(1)} %bitcast.154) | data formatting | bytes 4816896 | tf_op jit(solution)/shard_map/reshape | solution.py:78
  41.3 10.8 %copy.93 = bf16[2,1568,384]{2,0,1:T(2,128)(2,1)} copy(bf16[2,1568,384]{2,1,0:T(8,128)(2,1)S(1)} %bitcast.155) | data formatting | bytes 4816896 | tf_op jit(solution)/shard_map/reshape | solution.py:75
  116.7 25.7 %copy.94 = bf16[2,6272,384]{1,2,0:T(8,128)(2,1)} copy(bf16[2,6272,384]{2,0,1:T(2,128)(2,1)} %all-gather.4.cloned.1.call-done) | data formatting | bytes 19267584 | tf_op jit(solution)/shard_map/while | solution.py:111
  142.4 31.4 %all-gather.6.cloned.1.call-done = bf16[2,6272,384]{2,0,1:T(2,128)(2,1)} async-done(((bf16[2,1568,384]{2,0,1:T(2,128)(2,1)}), bf16[2,6272,384]{2,0,1:T(2,128)(2,1)}) %all-gather.6.cloned.1.call-update) | async-done | bytes 9633808 | tf_op jit(solution)/shard_map/all_gather | solution.py:80
  173.8 25.4 %copy.96 = bf16[2,6272,384]{1,2,0:T(8,128)(2,1)} copy(bf16[2,6272,384]{2,0,1:T(2,128)(2,1)} %all-gather.6.cloned.1.call-done) | data formatting | bytes 19267584 | tf_op jit(solution)/shard_map/while | solution.py:111
  199.3 114.7 %while.26 = (s32[]{:T(128)}, bf16[2,392,384]{2,1,0:T(8,128)(2,1)}, f32[2,4,392,1]{2,1,3,0:T(4,128)S(1)}, bf16[2,6272,384]{1,2,0:T(8,128)(2,1)}, pred[2,6272]{1,0...) while((s32[]{:T(128)}, bf16[2,392,384]{2,1,0:T(8,128)(2,1)}, ...), condition=%wide.region_7.8_spmd, body=%wide.region_4.7_spmd.sunk | while | flops 3894458880 | bytes 168170240 | solution.py:111
  206.2 15.8 %fusion.105 = (f32[4,392]{1,0:T(4,128)S(1)}, f32[4,392,6272]{2,1,0:T(8,128)}) fusion(pred[6272]{0:T(1024)(128)(4,1)S(1)} %dynamic-slice_reduce_fusion.4, bf16[6272,4,96]{0,2,1:T(8,128)(2,1)S(1)} %bitcast.146, bf16[2,392,4,96]{1,3,2,0:T(8,128)(2,1)S(1)} %get-tuple-element.485, s32[]{:T(128)} %get-tuple-element.472), kind=kOutput, calls=%fused_computation.3.clone.1 | convolution fusion | flops 1917725184 | bytes 44561540 | tf_op jit(solution)/shard_map/while/body/eval_jaxpr/qhd,khd->hqk/dot_general | solution.py:91
  222.0 17.7 %fusion.106 = f32[4,392]{1,0:T(4,128)S(1)} fusion(f32[4,392,6272]{2,1,0:T(8,128)} %get-tuple-element.448, f32[4,392]{1,0:T(4,128)S(1)} %get-tuple-element.449, pred[6272]{0:T(1024)(128)(4,1)S(1)} %dynamic-slice_reduce_fusion.4), kind=kLoop, calls=%fused_computation.4.clone.1 | loop fusion | flops 39336416 | bytes 39356800 | tf_op jit(solution)/shard_map/while/body/eval_jaxpr/reduce_sum | solution.py:101
  239.8 15.9 %fusion.107 = bf16[4,96,392]{2,1,0:T(8,128)(2,1)S(1)} fusion(bf16[6272,4,96]{0,2,1:T(8,128)(2,1)S(1)} %bitcast.149, f32[4,392,6272]{2,1,0:T(8,128)} %get-tuple-element.448, f32[4,392]{1,0:T(4,128)S(1)} %fusion.106, f32[4,392]{1,0:T(4,128)S(1)} %get-tuple-element.449, pred[6272]{0:T(1024)(128)(4,1)S(1)} %dynamic-slice_reduce_fusion.4), kind=kOutput, calls=%fused_computation.5.clone.1 | convolution fusion | flops 1937395712 | bytes 44474752 | tf_op jit(solution)/shard_map/while/body/eval_jaxpr/hqk,khd->qhd/dot_general | solution.py:103
  263.5 15.8 %fusion.105 = (f32[4,392]{1,0:T(4,128)S(1)}, f32[4,392,6272]{2,1,0:T(8,128)}) fusion(pred[6272]{0:T(1024)(128)(4,1)S(1)} %dynamic-slice_reduce_fusion.4, bf16[6272,4,96]{0,2,1:T(8,128)(2,1)S(1)} %bitcast.146, bf16[2,392,4,96]{1,3,2,0:T(8,128)(2,1)S(1)} %get-tuple-element.485, s32[]{:T(128)} %get-tuple-element.472), kind=kOutput, calls=%fused_computation.3.clone.1 | convolution fusion | flops 1917725184 | bytes 44561540 | tf_op jit(solution)/shard_map/while/body/eval_jaxpr/qhd,khd->hqk/dot_general | solution.py:91
  279.2 17.7 %fusion.106 = f32[4,392]{1,0:T(4,128)S(1)} fusion(f32[4,392,6272]{2,1,0:T(8,128)} %get-tuple-element.448, f32[4,392]{1,0:T(4,128)S(1)} %get-tuple-element.449, pred[6272]{0:T(1024)(128)(4,1)S(1)} %dynamic-slice_reduce_fusion.4), kind=kLoop, calls=%fused_computation.4.clone.1 | loop fusion | flops 39336416 | bytes 39356800 | tf_op jit(solution)/shard_map/while/body/eval_jaxpr/reduce_sum | solution.py:101
  297.0 15.9 %fusion.107 = bf16[4,96,392]{2,1,0:T(8,128)(2,1)S(1)} fusion(bf16[6272,4,96]{0,2,1:T(8,128)(2,1)S(1)} %bitcast.149, f32[4,392,6272]{2,1,0:T(8,128)} %get-tuple-element.448, f32[4,392]{1,0:T(4,128)S(1)} %fusion.106, f32[4,392]{1,0:T(4,128)S(1)} %get-tuple-element.449, pred[6272]{0:T(1024)(128)(4,1)S(1)} %dynamic-slice_reduce_fusion.4), kind=kOutput, calls=%fused_computation.5.clone.1 | convolution fusion | flops 1937395712 | bytes 44474752 | tf_op jit(solution)/shard_map/while/body/eval_jaxpr/hqk,khd->qhd/dot_general | solution.py:103
  316.5 13.2 %multiply_convert_fusion.1 = (bf16[784,1536]{1,0:T(8,128)(2,1)}, f32[784,1536]{1,0:T(8,128)S(1)}, f32[784,1536]{1,0:T(8,128)S(1)}) fusion(f32[1536]{0:T(1024)S(1)} %copy-done.43, bf16[384,1536]{1,0:T(8,128)(2,1)S(1)} %copy-done, f32[784,384]{1,0:T(8,128)S(1)} %get-tuple-element.330, f32[384]{0:T(512)S(1)} %copy-done.40, f32[384]{0:T(512)S(1)} %copy-done.37, ...), kind=kOutput, calls=%fused_computation.57 | convolution fusion | flops 1005828096 | bytes 14441600 | tf_op jit(solution)/shard_map/dot_general | solution.py:119
  365.6 297.4 %while.27 = (s32[]{:T(128)}, f32[2,392,384]{1,2,0:T(8,128)}, bf16[2,6272,384]{2,1,0:T(8,128)(2,1)}, bf16[2,6272,384]{2,1,0:T(8,128)(2,1)}, bf16[2,6272,384]{1,2,...) while((s32[]{:T(128)}, f32[2,392,384]{1,2,0:T(8,128)}, ...), condition=%wide.region_14.15_spmd, body=%wide.region_12.14_spmd.sunk | while | flops 9593600000 | bytes 414286016 | solution.py:185
  368.5 15.5 %fusion.117 = f32[4,392,6272]{2,1,0:T(8,128)} fusion(bf16[6272,4,96]{0,2,1:T(8,128)(2,1)S(1)} %bitcast.141, bf16[2,392,4,96]{1,3,2,0:T(8,128)(2,1)S(1)} %get-tuple-element.516, s32[]{:T(128)} %get-tuple-element.499), kind=kOutput, calls=%fused_computation.29.clone.1 | convolution fusion | flops 1888223232 | bytes 44548100 | tf_op jit(solution)/shard_map/while/body/eval_jaxpr/qhd,khd->hqk/dot_general | solution.py:91
  389.0 27.7 %multiply_reduce_fusion.8 = (f32[4,392]{1,0:T(4,128)S(1)}, f32[4,392,6272]{2,1,0:T(8,128)}) fusion(f32[4,392,6272]{2,1,0:T(8,128)} %fusion.117, f32[4,392]{1,0:T(4,128)S(1)} %dynamic-slice_bitcast_fusion.2, pred[6272]{0:T(1024)(128)(4,1)S(1)} %dynamic-slice_reduce_fusion.5, bf16[6272,4,96]{0,2,1:T(8,128)(2,1)} %bitcast.147, ...), kind=kOutput, calls=%fused_computation.18.clone.1 | convolution fusion | flops 1937394176 | bytes 83907712 | tf_op jit(solution)/shard_map/while/body/eval_jaxpr/qhd,khd->hqk/dot_general | solution.py:148
  416.7 33.0 %multiply_convert_fusion.5 = bf16[4,392,6272]{2,1,0:T(8,128)(2,1)} fusion(f32[4,392,6272]{2,1,0:T(8,128)} %get-tuple-element.460, f32[4,392,6272]{2,1,0:T(8,128)} %fusion.117, f32[4,392]{1,0:T(4,128)S(1)} %get-tuple-element.461, f32[4,392]{1,0:T(4,128)S(1)} %dynamic-slice_bitcast_fusion.2, pred[6272]{0:T(1024)(128)(4,1)S(1)} %dynamic-slice_reduce_fusion.5), kind=kLoop, calls=%fused_computation.17.clone.1 | loop fusion | flops 59006976 | bytes 98363776 | tf_op jit(solution)/shard_map/while/body/eval_jaxpr/convert_element_type | solution.py:159
  449.8 12.7 %convolution_multiply_fusion.5 = bf16[4,96,6272]{2,1,0:T(8,128)(2,1)} fusion(bf16[4,392,6272]{2,1,0:T(8,128)(2,1)} %multiply_convert_fusion.5, bf16[2,392,4,96]{1,3,2,0:T(8,128)(2,1)S(1)} %get-tuple-element.516, s32[]{:T(128)} %get-tuple-element.499), kind=kOutput, calls=%fused_computation.23.clone.1 | convolution fusion | flops 1893040128 | bytes 24879108 | tf_op jit(solution)/shard_map/while/body/eval_jaxpr/hqk,qhd->khd/dot_general | solution.py:170
  470.0 18.3 %fusion.118 = bf16[4,96,6272]{2,1,0:T(8,128)(2,1)} fusion(f32[4,392,6272]{2,1,0:T(8,128)} %fusion.117, f32[4,392]{1,0:T(4,128)S(1)} %dynamic-slice_bitcast_fusion.2, pred[6272]{0:T(1024)(128)(4,1)S(1)} %dynamic-slice_reduce_fusion.5, bf16[2,392,4,96]{1,3,2,0:T(8,128)(2,1)S(1)} %get-tuple-element.518, s32[]{:T(128)} %get-tuple-element.499), kind=kOutput, calls=%fused_computation.21.clone.1 | convolution fusion | flops 1927561216 | bytes 44563460 | tf_op jit(solution)/shard_map/while/body/eval_jaxpr/hqk,qhd->khd/dot_general | solution.py:173
  496.0 8.5 constant_dynamic-update-slice_fusion.9
  504.5 9.6 %convolution_multiply_fusion.4 = f32[4,96,392]{2,1,0:T(8,128)S(1)} fusion(bf16[6272,4,96]{0,2,1:T(8,128)(2,1)S(1)} %bitcast.144, bf16[4,392,6272]{2,1,0:T(8,128)(2,1)} %multiply_convert_fusion.5), kind=kOutput, calls=%fused_computation.24.clone.1 | convolution fusion | flops 1888373760 | bytes 25088000 | tf_op jit(solution)/shard_map/while/body/eval_jaxpr/hqk,khd->qhd/dot_general | solution.py:161
  517.8 15.4 %fusion.117 = f32[4,392,6272]{2,1,0:T(8,128)} fusion(bf16[6272,4,96]{0,2,1:T(8,128)(2,1)S(1)} %bitcast.141, bf16[2,392,4,96]{1,3,2,0:T(8,128)(2,1)S(1)} %get-tuple-element.516, s32[]{:T(128)} %get-tuple-element.499), kind=kOutput, calls=%fused_computation.29.clone.1 | convolution fusion | flops 1888223232 | bytes 44548100 | tf_op jit(solution)/shard_map/while/body/eval_jaxpr/qhd,khd->hqk/dot_general | solution.py:91
  538.2 27.5 %multiply_reduce_fusion.8 = (f32[4,392]{1,0:T(4,128)S(1)}, f32[4,392,6272]{2,1,0:T(8,128)}) fusion(f32[4,392,6272]{2,1,0:T(8,128)} %fusion.117, f32[4,392]{1,0:T(4,128)S(1)} %dynamic-slice_bitcast_fusion.2, pred[6272]{0:T(1024)(128)(4,1)S(1)} %dynamic-slice_reduce_fusion.5, bf16[6272,4,96]{0,2,1:T(8,128)(2,1)} %bitcast.147, ...), kind=kOutput, calls=%fused_computation.18.clone.1 | convolution fusion | flops 1937394176 | bytes 83907712 | tf_op jit(solution)/shard_map/while/body/eval_jaxpr/qhd,khd->hqk/dot_general | solution.py:148
  565.7 31.7 %multiply_convert_fusion.5 = bf16[4,392,6272]{2,1,0:T(8,128)(2,1)} fusion(f32[4,392,6272]{2,1,0:T(8,128)} %get-tuple-element.460, f32[4,392,6272]{2,1,0:T(8,128)} %fusion.117, f32[4,392]{1,0:T(4,128)S(1)} %get-tuple-element.461, f32[4,392]{1,0:T(4,128)S(1)} %dynamic-slice_bitcast_fusion.2, pred[6272]{0:T(1024)(128)(4,1)S(1)} %dynamic-slice_reduce_fusion.5), kind=kLoop, calls=%fused_computation.17.clone.1 | loop fusion | flops 59006976 | bytes 98363776 | tf_op jit(solution)/shard_map/while/body/eval_jaxpr/convert_element_type | solution.py:159
  597.4 12.7 %convolution_multiply_fusion.5 = bf16[4,96,6272]{2,1,0:T(8,128)(2,1)} fusion(bf16[4,392,6272]{2,1,0:T(8,128)(2,1)} %multiply_convert_fusion.5, bf16[2,392,4,96]{1,3,2,0:T(8,128)(2,1)S(1)} %get-tuple-element.516, s32[]{:T(128)} %get-tuple-element.499), kind=kOutput, calls=%fused_computation.23.clone.1 | convolution fusion | flops 1893040128 | bytes 24879108 | tf_op jit(solution)/shard_map/while/body/eval_jaxpr/hqk,qhd->khd/dot_general | solution.py:170
  617.6 18.3 %fusion.118 = bf16[4,96,6272]{2,1,0:T(8,128)(2,1)} fusion(f32[4,392,6272]{2,1,0:T(8,128)} %fusion.117, f32[4,392]{1,0:T(4,128)S(1)} %dynamic-slice_bitcast_fusion.2, pred[6272]{0:T(1024)(128)(4,1)S(1)} %dynamic-slice_reduce_fusion.5, bf16[2,392,4,96]{1,3,2,0:T(8,128)(2,1)S(1)} %get-tuple-element.518, s32[]{:T(128)} %get-tuple-element.499), kind=kOutput, calls=%fused_computation.21.clone.1 | convolution fusion | flops 1927561216 | bytes 44563460 | tf_op jit(solution)/shard_map/while/body/eval_jaxpr/hqk,qhd->khd/dot_general | solution.py:173
  643.6 8.6 constant_dynamic-update-slice_fusion.9
  652.2 9.6 %convolution_multiply_fusion.4 = f32[4,96,392]{2,1,0:T(8,128)S(1)} fusion(bf16[6272,4,96]{0,2,1:T(8,128)(2,1)S(1)} %bitcast.144, bf16[4,392,6272]{2,1,0:T(8,128)(2,1)} %multiply_convert_fusion.5), kind=kOutput, calls=%fused_computation.24.clone.1 | convolution fusion | flops 1888373760 | bytes 25088000 | tf_op jit(solution)/shard_map/while/body/eval_jaxpr/hqk,khd->qhd/dot_general | solution.py:161
  690.8 52.0 %reduce-scatter.14.cloned.1.call-done = bf16[2,1568,384]{2,1,0:T(8,128)(2,1)} async-done(((bf16[2,6272,384]{2,1,0:T(8,128)(2,1)}), bf16[2,1568,384]{2,1,0:T(8,128)(2,1)}) %reduce-scatter.14.cloned.1.call-update) | async-done | bytes 2408464 | tf_op jit(solution)/shard_map/reduce_scatter | solution.py:189
  742.8 82.5 %reduce-scatter.16.cloned.1.call-done = bf16[2,1568,384]{2,1,0:T(8,128)(2,1)} async-done(((bf16[2,6272,384]{2,1,0:T(8,128)(2,1)}), bf16[2,1568,384]{2,1,0:T(8,128)(2,1)}) %reduce-scatter.16.cloned.1.call-update) | async-done | bytes 2408464 | tf_op jit(solution)/shard_map/reduce_scatter | solution.py:192
  855.1 10.1 %all-reduce.11 = (bf16[192]{0:T(256)(128)(2,1)S(1)}, bf16[192]{0:T(256)(128)(2,1)S(1)}, bf16[384]{0:T(512)(128)(2,1)S(1)}, bf16[384]{0:T(512)(128)(2,1)S(1)}, bf...) all-reduce(bf16[192]{0:T(256)(128)(2,1)S(1)} %get-tuple-element.243, ...), channel_id=4, replica_groups=mesh['clip'=8,'unit'=4] {'unit'}, use_global_device_ids=true, to_apply=%region_20.21.clone | all-reduce | flops 4608 | bytes 18432
  866.7 86.1 %all-reduce.13 = (f32[48]{0:T(128)}, f32[48]{0:T(128)}, f32[192,96]{1,0:T(8,128)}, f32[96]{0:T(128)}, f32[192,288]{1,0:T(8,128)}, /*index=5*/f32[96]{0:T(128)}, ...) all-reduce(f32[48]{0:T(128)S(1)} %get-tuple-element.343, ...), channel_id=1, replica_groups=mesh['clip'=8,'unit'=4] {'clip'}, use_global_device_ids=true, to_apply=%region_21.22 | all-reduce | flops 406656 | bytes 2442240 | tf_op jit(solution)/shard_map/psum | solution.py:267
  (288 shorter events, 245.9 us)
Async XLA Ops:
  7.2 309.3 %copy-start = (bf16[384,1536]{1,0:T(8,128)(2,1)S(1)}, bf16[384,1536]{1,0:T(8,128)(2,1)}, u32[]{:S(2)}) copy-start(bf16[384,1536]{1,0:T(8,128)(2,1)} %param.35) | copy-start | bytes 3538948
  7.2 109.5 %all-gather.4.cloned.1.call-start = ((), (), s32[]{:S(2)}) async-start(), calls=%async_computation.7 | async-start | bytes 12042240 | tf_op jit(solution)/shard_map/all_gather | solution.py:81
  8.0 79.5 %copy-start.38 = (f32[192]{0:T(256)}, f32[192]{0:T(256)S(1)}, u32[]{:S(2)}) copy-start(f32[192]{0:T(256)S(1)} %convert_element_type.194) | copy-start | bytes 2308
  12.5 75.0 %copy-start.41 = (f32[192]{0:T(256)}, f32[192]{0:T(256)S(1)}, u32[]{:S(2)}) copy-start(f32[192]{0:T(256)S(1)} %convert_element_type.195) | copy-start | bytes 2308
  38.6 135.2 %all-gather.6.cloned.1.call-start = ((), (), s32[]{:S(2)}) async-start(), calls=%async_computation.8 | async-start | bytes 12042240 | tf_op jit(solution)/shard_map/all_gather | solution.py:80
  52.2 636.5 %reduce-scatter.22.cloned.1.call-start = ((), (), s32[]{:S(2)}) async-start(), calls=%async_computation.13 | async-start | bytes 245760
  99.6 15.0 %copy-start.46 = (bf16[1536]{0:T(1024)(128)(2,1)S(1)}, bf16[1536]{0:T(1024)(128)(2,1)}, u32[]{:S(2)}) copy-start(bf16[1536]{0:T(1024)(128)(2,1)} %param.36) | copy-start | bytes 9220
  99.6 15.6 %copy-start.54 = (bf16[384]{0:T(512)(128)(2,1)S(1)}, bf16[384]{0:T(512)(128)(2,1)}, u32[]{:S(2)}) copy-start(bf16[384]{0:T(512)(128)(2,1)} %param.34) | copy-start | bytes 2308
  99.6 16.1 %copy-start.18 = (bf16[2,98,4,384]{3,2,1,0:T(4,128)(2,1)S(1)}, bf16[2,98,4,384]{3,2,1,0:T(4,128)(2,1)}, u32[]{:S(2)}) copy-start(bf16[2,98,4,384]{3,2,1,0:T(4,128)(2,1)} %param.41) | copy-start | bytes 1806340
  199.2 114.7 %copy-start.23 = (bf16[384,384]{1,0:T(8,128)(2,1)S(1)}, bf16[384,384]{1,0:T(8,128)(2,1)}, u32[]{:S(2)}) copy-start(bf16[384,384]{1,0:T(8,128)(2,1)} %param.31) | copy-start | bytes 884740
  199.2 114.7 %copy-start.44 = (f32[384]{0:T(512)S(1)}, f32[384]{0:T(512)}, u32[]{:S(2)}) copy-start(f32[384]{0:T(512)} %convert_element_type.204) | copy-start | bytes 4612
  199.2 117.2 %copy-start.37 = (f32[384]{0:T(512)S(1)}, f32[384]{0:T(512)}, u32[]{:S(2)}) copy-start(f32[384]{0:T(512)} %convert_element_type.205) | copy-start | bytes 4612
  199.2 117.3 %copy-start.40 = (f32[384]{0:T(512)S(1)}, f32[384]{0:T(512)}, u32[]{:S(2)}) copy-start(f32[384]{0:T(512)} %convert_element_type.206) | copy-start | bytes 4612
  199.2 117.3 %copy-start.43 = (f32[1536]{0:T(1024)S(1)}, f32[1536]{0:T(1024)}, u32[]{:S(2)}) copy-start(f32[1536]{0:T(1024)} %convert_element_type.208) | copy-start | bytes 18436
  222.0 17.8 %copy-start.3 = (bf16[1,6272,384]{1,2,0:T(8,128)(2,1)S(1)}, bf16[1,6272,384]{1,2,0:T(8,128)(2,1)}, u32[]{:S(2)}) copy-start(bf16[1,6272,384]{1,2,0:T(8,128)(2,1)} %get-tuple-element.446) | copy-start | bytes 14450692 | tf_op jit(solution)/shard_map/while
  279.2 17.8 %copy-start.3 = (bf16[1,6272,384]{1,2,0:T(8,128)(2,1)S(1)}, bf16[1,6272,384]{1,2,0:T(8,128)(2,1)}, u32[]{:S(2)}) copy-start(bf16[1,6272,384]{1,2,0:T(8,128)(2,1)} %get-tuple-element.446) | copy-start | bytes 14450692 | tf_op jit(solution)/shard_map/while
  313.9 15.8 %copy-start.14 = (pred[2,6272]{1,0:T(4,128)(4,1)}, pred[2,6272]{1,0:T(4,128)(4,1)S(1)}, u32[]{:S(2)}) copy-start(pred[2,6272]{1,0:T(4,128)(4,1)S(1)} %get-tuple-element.545) | copy-start | bytes 37636
  316.1 19.7 %copy-start.8 = (f32[784,384]{1,0:T(8,128)}, f32[784,384]{1,0:T(8,128)S(1)}, u32[]{:S(2)}) copy-start(f32[784,384]{1,0:T(8,128)S(1)} %get-tuple-element.330) | copy-start | bytes 3612676
  350.5 339.1 %reduce-scatter.18.cloned.1.call-start = ((), (), s32[]{:S(2)}) async-start(), calls=%async_computation.11 | async-start | bytes 368640 | tf_op jit(solution)/shard_map/reduce_scatter | solution.py:242
  351.9 337.7 %reduce-scatter.26.cloned.1.call-start = ((), (), s32[]{:S(2)}) async-start(), calls=%async_computation.15 | async-start | bytes 1474560
  359.1 331.7 %reduce-scatter.20.cloned.1.call-start = ((), (), s32[]{:S(2)}) async-start(), calls=%async_computation.12 | async-start | bytes 1474560 | tf_op jit(solution)/shard_map/reduce_scatter | solution.py:260
  365.5 377.2 %reduce-scatter.14.cloned.1.call-start = ((), (), s32[]{:S(2)}) async-start(), calls=%async_computation.9 | async-start | bytes 12042240 | tf_op jit(solution)/shard_map/reduce_scatter | solution.py:189
  368.5 15.5 %copy-start.2 = (bf16[1,6272,384]{1,2,0:T(8,128)(2,1)}, bf16[1,6272,384]{1,2,0:T(8,128)(2,1)S(1)}, u32[]{:S(2)}) copy-start(bf16[1,6272,384]{1,2,0:T(8,128)(2,1)S(1)} %constant_dynamic-slice_fusion.8) | copy-start | bytes 14450692 | tf_op jit(solution)/shard_map/while
  488.3 16.2 %slice-start = ((s8[4816896]{0:T(1024)(128)(4,1)}), s8[622592]{0:T(1024)(128)(4,1)S(1)}, s32[]{:S(2)}) async-start(s8[4816896]{0:T(1024)(128)(4,1)} %bitcast.142), calls=%async_computation.16 | async-start | bytes 1245184 | tf_op jit(solution)/shard_map/while
  517.8 15.4 %copy-start.2 = (bf16[1,6272,384]{1,2,0:T(8,128)(2,1)}, bf16[1,6272,384]{1,2,0:T(8,128)(2,1)S(1)}, u32[]{:S(2)}) copy-start(bf16[1,6272,384]{1,2,0:T(8,128)(2,1)S(1)} %constant_dynamic-slice_fusion.8) | copy-start | bytes 14450692 | tf_op jit(solution)/shard_map/while
  636.0 16.2 %slice-start = ((s8[4816896]{0:T(1024)(128)(4,1)}), s8[622592]{0:T(1024)(128)(4,1)S(1)}, s32[]{:S(2)}) async-start(s8[4816896]{0:T(1024)(128)(4,1)} %bitcast.142), calls=%async_computation.16 | async-start | bytes 1245184 | tf_op jit(solution)/shard_map/while
  663.0 162.3 %reduce-scatter.16.cloned.1.call-start = ((), (), s32[]{:S(2)}) async-start(), calls=%async_computation.10 | async-start | bytes 12042240 | tf_op jit(solution)/shard_map/reduce_scatter | solution.py:192
  663.8 201.9 %reduce-scatter.24.cloned.1.call-start = ((), (), s32[]{:S(2)}) async-start(), calls=%async_computation.14 | async-start | bytes 737280
  679.4 145.9 %copy-start.30 = (bf16[192,1152]{1,0:T(8,128)(2,1)S(1)}, bf16[192,1152]{1,0:T(8,128)(2,1)}, u32[]{:S(2)}) copy-start(bf16[192,1152]{1,0:T(8,128)(2,1)} %param.28) | copy-start | bytes 1327108
  848.0 18.7 %copy-start.33 = (bf16[384,384]{1,0:T(8,128)(2,1)S(1)}, bf16[384,384]{1,0:T(8,128)(2,1)}, u32[]{:S(2)}) copy-start(bf16[384,384]{1,0:T(8,128)(2,1)} %reduce-scatter.20.cloned.1.call-done) | copy-start | bytes 884740
  848.0 18.7 %copy-start.36 = (bf16[384,96]{0,1:T(8,128)(2,1)S(1)}, bf16[384,96]{0,1:T(8,128)(2,1)}, u32[]{:S(2)}) copy-start(bf16[384,96]{0,1:T(8,128)(2,1)} %reduce-scatter.18.cloned.1.call-done) | copy-start | bytes 221188
  848.0 104.9 %copy-start.1 = (bf16[384,1536]{1,0:T(8,128)(2,1)S(1)}, bf16[384,1536]{1,0:T(8,128)(2,1)}, u32[]{:S(2)}) copy-start(bf16[384,1536]{1,0:T(8,128)(2,1)} %param.35) | copy-start | bytes 3538948
  (45 other events, 340.2 us)
Sparse Core Ops, SparseCore 0:
  38.7 68.0 all-gather.3
  108.4 65.3 all-gather.5
  350.6 19.7 reduce-scatter.21
  373.3 20.2 reduce-scatter.17
  396.2 25.6 reduce-scatter.25
  424.4 25.7 reduce-scatter.19
  663.1 79.5 reduce-scatter.13
  745.6 79.6 reduce-scatter.15
  837.2 22.0 reduce-scatter.23
where the time goes:
time: 971 us; the launch traced here: 960 us
  matrix products  289 us (30%)
  local copies, waits for them, and re-layouts  233 us (24%)
  waiting for transfers between devices  167 us (17%)
  other arithmetic  151 us (16%)
  blocking collectives  103 us (11%)
  between operations  17.1 us (2%)
    psum x1, blocking collectives, shards(): lax.psum((shares[0], shares[1], shares[2], shares[3], shares[4], shares[5...  86.1 us
    reduce_scatter x1, waiting for transfers between devices, shards(): lax.psum_scatter(value_grad_all.astype(jnp.bfloat16), 'unit', scatter_dim...  82.5 us
    convert_element_type x2, other arithmetic, attend_back(): score_grad = (probability * (probs_grad - row_inner)).astype(jnp.bfloat16)  64.7 us
    dot_general x4, matrix products, clip_scores(): jnp.einsum('qhd,khd->hqk', query_one, key_heads, preferred_element_type=j...  62.4 us
    dot_general x2, matrix products, score_grads(): jnp.einsum('qhd,khd->hqk', grad_one, value_heads, preferred_element_type=...  55.2 us
    while x3, local copies, waits for them, and re-layouts, shards(): lax.map(attend, (query_heads, key_rows, value_rows, key_valid))  52.6 us
    reduce_scatter x1, waiting for transfers between devices, shards(): lax.psum_scatter(key_grad_all.astype(jnp.bfloat16), 'unit', scatter_dimen...  52 us
    dynamic_update_slice x6, local copies, waits for them, and re-layouts, shards(): lax.map(attend_back, (query_heads, key_rows, value_rows, key_valid, log_t...  47.6 us
  transfers between devices with their start and end apart: 9, of which 3 were waited for; matrix products, arithmetic and copies ran while one was open for 47% of the time, Pallas kernels for 0%

commit v1 on v0

v1 whole, which is shorter than its diff:
```python
import functools

import jax
import jax.numpy as jnp
from jax import lax
from jax.experimental import pallas as pl
from jax.experimental.pallas import tpu as pltpu
from jax.sharding import PartitionSpec as P

D_IN = 192
D_OUT = 384
HEADS = 4
HEAD_DIM = 96
FF = 1536
LANES = 128
EXT = 208
SCALE = HEAD_DIM**-0.5
LOG2E = 1.4426950408889634
BF = jnp.bfloat16
F32 = jnp.float32
VMEM_BYTES = 60 * 2**20


def mm(a, b, ca, cb):
    return lax.dot_general(a, b, (((ca,), (cb,)), ((), ())), preferred_element_type=F32)


def iota(shape, dim):
    return lax.broadcasted_iota(jnp.int32, shape, dim)


def call(body, grid, ins, outs, scratch=(), name=None, cost=None, after=()):
    count = len(ins)

    def run(*refs):
        body(*refs[:count], *refs[count + len(after) :])

    ins = [*ins, *((pl.BlockSpec(memory_space=pl.ANY), value) for value in after)]
    return pl.pallas_call(
        run,
        grid=grid,
        in_specs=[spec for spec, _ in ins],
        out_specs=[spec for spec, _, _ in outs],
        out_shape=[jax.ShapeDtypeStruct(shape, dtype) for _, shape, dtype in outs],
        scratch_shapes=list(scratch),
        compiler_params=pltpu.CompilerParams(
            dimension_semantics=("arbitrary",) * len(grid), vmem_limit_bytes=VMEM_BYTES
        ),
        name=name,
        cost_estimate=pl.CostEstimate(
            flops=int(cost * 1.1e9), bytes_accessed=int(cost * 1e6), transcendentals=0
        ),
    )(*[value for _, value in ins])


def whole(value):
    rank = len(value.shape)
    return (pl.BlockSpec(value.shape, lambda *_: (0,) * rank), value)


def part(value):
    rank = len(value.shape)
    return (pl.BlockSpec((1,) + value.shape[1:], lambda i: (i,) + (0,) * (rank - 1)), value)


def at_clip(value, clip):
    rank = len(value.shape)
    return (pl.BlockSpec((1,) + value.shape[1:], lambda *_: (clip,) + (0,) * (rank - 1)), value)


def at_head(value, clip):
    rank = len(value.shape)
    return (
        pl.BlockSpec((None, 1) + value.shape[2:], lambda i: (clip, i) + (0,) * (rank - 2)),
        value,
    )


def out_part(shape, dtype):
    rank = len(shape)
    return (pl.BlockSpec((1,) + shape[1:], lambda i: (i,) + (0,) * (rank - 1)), shape, dtype)


def out_whole(shape, dtype):
    rank = len(shape)
    return (pl.BlockSpec(shape, lambda *_: (0,) * rank), shape, dtype)


V_GAIN1, V_SHIFT1, V_PROJ, V_OUT, V_GAIN2, V_SHIFT2, V_SHRINK, V_EXPAND, V_QKV = range(9)


def vec(table, row, width):
    return table[row : row + 1, :width]


def normed_body(tok_ref, inv_ref, cols_ref, nt_ref, pooled_ref):
    slots, _, units = tok_ref.shape[1:]
    gain, shift = cols_ref[:, 0:1], cols_ref[:, 1:2]
    pieces = []
    for s in range(slots):
        x = tok_ref[0, s].astype(F32)
        center = x - jnp.mean(x, axis=0, keepdims=True)
        var = jnp.mean(center * center, axis=0, keepdims=True)
        pieces.append((center * lax.rsqrt(var + 1e-06) * gain + shift).astype(BF).astype(F32))
    nt_ref[:D_IN, :] = jnp.concatenate(pieces, axis=1).astype(BF)
    extra = iota((EXT - D_IN, units), 0)
    extra = jnp.where(extra == 0, 1.0, jnp.where(extra == 1, inv_ref[0], 0.0))
    nt_ref[D_IN:, :] = jnp.concatenate([extra] * slots, axis=1).astype(BF)
    means = []
    for p in range(4):
        first = 8 * (p >> 1) + 2 * (p & 1)
        means.append(
            (pieces[first] + pieces[first + 1] + pieces[first + 4] + pieces[first + 5]) * 0.25
        )
    pooled = jnp.concatenate(means, axis=1)
    row = iota((2 * LANES - D_IN, 4 * units), 0)
    pooled = jnp.concatenate([pooled, jnp.where(row == 0, 1.0, 0.0)], axis=0)
    pooled_ref[...] = pooled.T.astype(BF)


def normed_tokens(clip, tokens, invalid, cols):
    _, slots, _, units = tokens.shape
    return call(
        normed_body,
        (1,),
        [at_clip(tokens, clip), at_clip(invalid, clip), whole(cols)],
        [out_whole((EXT, slots * units), BF), out_whole((4 * units, 2 * LANES), BF)],
        name="normed",
        cost=3,
    )


def query_body(clips, qkv_ref, wp_ref, table_ref, *refs):
    pooled_refs, wt_ref, q_refs = refs[:clips], refs[clips], refs[clips + 1 :]
    bias = jnp.where(
        iota((EXT - D_IN, 3 * D_OUT), 0) == 0, vec(table_ref, V_QKV, 3 * D_OUT), 0.0
    ).astype(BF)
    extended = jnp.concatenate([qkv_ref[...], bias], axis=0)
    eye = jnp.where(iota((LANES, HEAD_DIM), 0) == iota((LANES, HEAD_DIM), 1), 1.0, 0.0).astype(BF)
    row, lane = iota((LANES, EXT), 0), iota((LANES, EXT), 1)
    ones = (lane == D_IN) & (row >= HEAD_DIM)
    extras = (
        jnp.where(ones & (row == HEAD_DIM), 8.0, 0.0),
        jnp.where((lane == D_IN + 1) & (row == HEAD_DIM), -1e30, 0.0),
        jnp.where(ones & (row <= HEAD_DIM + 1), 1.0, 0.0),
    )
    for block in range(3 * HEADS):
        columns = extended[:, HEAD_DIM * block : HEAD_DIM * (block + 1)]
        wt_ref[block, :, :EXT] = (mm(eye, columns, 1, 1) + extras[block // HEADS]).astype(BF)
        wt_ref[block, :, EXT:] = jnp.zeros((LANES, 2 * LANES - EXT), BF)
    eye = jnp.where(iota((LANES, LANES), 0) == iota((LANES, LANES), 1), 1.0, 0.0).astype(BF)
    for block in range(D_OUT // LANES):
        columns = wp_ref[:, LANES * block : LANES * (block + 1)]
        wt_ref[3 * HEADS + block, :, :D_IN] = mm(eye, columns, 1, 1).astype(BF)
        wt_ref[3 * HEADS + block, :, D_IN:] = jnp.zeros((LANES, 2 * LANES - D_IN), BF)
    for c in range(clips):
        pooled = pooled_refs[c][...]
        for h in range(HEADS):
            q_refs[2 * c][h] = (mm(pooled, wt_ref[h], 1, 1) * (SCALE * LOG2E)).astype(BF)
            q_refs[2 * c + 1][h] = (mm(wt_ref[h, :HEAD_DIM], pooled, 1, 1) * SCALE).astype(BF)


def queries_of(qkv, wp, table, pooled):
    clips, count = len(pooled), pooled[0].shape[0]
    wt, *rest = call(
        functools.partial(query_body, clips),
        (1,),
        [whole(qkv), whole(wp), whole(table), *(whole(value) for value in pooled)],
        [
            out_whole((3 * HEADS + D_OUT // LANES, LANES, 2 * LANES), BF),
            *[
                out_whole((HEADS, count, LANES), BF),
                out_whole((HEADS, HEAD_DIM, count), BF),
            ]
            * clips,
        ],
        name="queries",
        cost=5,
    )
    return wt, [(rest[2 * c], rest[2 * c + 1]) for c in range(clips)]


def forward_body(na_ref, nb_ref, wt_ref, qs_ref, p_ref, kt_ref, vt_ref, o_ref, n_ref):
    rows = na_ref.shape[1]

    @pl.when(pl.program_id(0) == 0)
    def _():
        n_ref[:, :rows] = na_ref[...]
        n_ref[:, rows:] = nb_ref[...]

    n = n_ref[...]
    h = pl.program_id(0)
    kt = mm(wt_ref[HEADS + h][:, :EXT], n, 1, 0).astype(BF)
    vt = mm(wt_ref[2 * HEADS + h][:, :EXT], n, 1, 0).astype(BF)
    kt_ref[0] = kt
    vt_ref[0] = vt
    s = mm(qs_ref[0], kt, 1, 0)
    m = jnp.max(s, axis=1, keepdims=True)
    p = jnp.exp2(s - m).astype(BF)
    p_ref[0] = p
    o = mm(p, vt, 1, 1)
    o_ref[0] = jnp.where(iota(o.shape, 1) == HEAD_DIM + 1, m, o)


def forward(na, nb, wt, qs, after=()):
    rows = na.shape[1]
    queries = qs.shape[1]
    return call(
        forward_body,
        (HEADS,),
        [whole(na), whole(nb), whole(wt), part(qs)],
        [
            out_part((HEADS, queries, 2 * rows), BF),
            out_part((HEADS, LANES, 2 * rows), BF),
            out_part((HEADS, LANES, 2 * rows), BF),
            out_part((HEADS, queries, LANES), F32),
        ],
        [pltpu.VMEM((EXT, 2 * rows), BF)],
        name="attend",
        after=after,
        cost=16,
    )


def middle_body(clips, me_ref, *refs):
    o1_refs, o2_refs, pooled_refs = refs[:clips], refs[clips : 2 * clips], refs[2 * clips : 3 * clips]
    for c in range(clips):

        @pl.when(pl.program_id(0) == c)
        def _():
            middle_clip(
                clips, c, me_ref, o1_refs[c], o2_refs[c], pooled_refs[c], *refs[3 * clips :]
            )


def middle_clip(
    clips,
    step,
    me_ref,
    o1_ref,
    o2_ref,
    pooled_ref,
    up_ref,
    table_ref,
    wp_ref,
    wo_ref,
    we_ref,
    ws_ref,
    out_ref,
    hg_ref,
    do1_ref,
    do2_ref,
    do1t_ref,
    do2t_ref,
    keep_ref,
    send_ref,
    wpt_ref,
    we_acc,
    ws_acc,
    wo_acc,
    wp_acc,
    misc_acc,
):
    queries = pooled_ref.shape[0]
    pooled = pooled_ref[...]
    up_low = up_ref[0]
    up = up_low.astype(F32)

    if step == 0:
        we_acc[...] = jnp.zeros_like(we_acc)
        ws_acc[...] = jnp.zeros_like(ws_acc)
        wo_acc[...] = jnp.zeros_like(wo_acc)
        wp_acc[...] = jnp.zeros_like(wp_acc)
        misc_acc[...] = jnp.zeros_like(misc_acc)

    heads = []
    factors = []
    for h in range(HEADS):
        o1, o2 = o1_ref[h], o2_ref[h]
        l1, l2 = o1[:, HEAD_DIM : HEAD_DIM + 1], o2[:, HEAD_DIM : HEAD_DIM + 1]
        m1, m2 = o1[:, HEAD_DIM + 1 : HEAD_DIM + 2], o2[:, HEAD_DIM + 1 : HEAD_DIM + 2]
        m = jnp.maximum(m1, m2)
        a1, a2 = jnp.exp2(m1 - m), jnp.exp2(m2 - m)
        inverse = 1.0 / (a1 * l1 + a2 * l2)
        c1, c2 = a1 * inverse, a2 * inverse
        heads.append(o1[:, :HEAD_DIM] * c1 + o2[:, :HEAD_DIM] * c2)
        factors.append((c1, c2))
    attended = jnp.concatenate(heads, axis=1)
    attended_low = attended.astype(BF)
    hidden = mm(pooled[:, :D_IN], wp_ref[...], 1, 0) + vec(table_ref, V_PROJ, D_OUT)
    hidden = hidden + mm(attended_low, wo_ref[...], 1, 0) + vec(table_ref, V_OUT, D_OUT)
    center = hidden - jnp.mean(hidden, axis=1, keepdims=True)
    inv_std = lax.rsqrt(jnp.mean(center * center, axis=1, keepdims=True) + 1e-06)
    n = center * inv_std
    gain2 = vec(table_ref, V_GAIN2, D_OUT)
    second = (n * gain2 + vec(table_ref, V_SHIFT2, D_OUT)).astype(BF)
    before = mm(second, we_ref[...], 1, 0) + vec(table_ref, V_EXPAND, FF)
    cdf = 0.5 + 0.5 * lax.erf(before * (0.5**0.5))
    active = (before * cdf).astype(BF)
    out_ref[0] = hidden + mm(active, ws_ref[...], 1, 0) + vec(table_ref, V_SHRINK, D_OUT)
    slope = cdf + before * (jnp.exp(before * before * -0.5) * (0.5 / jnp.pi) ** 0.5)
    before_grad = (mm(up_low, ws_ref[...], 1, 1) * slope).astype(BF)
    ws_acc[...] += mm(up_low, active, 0, 0)
    we_acc[...] += mm(second, before_grad, 0, 0)
    second_grad = mm(before_grad, we_ref[...], 1, 1)
    e = gain2 * second_grad
    back = (
        e - jnp.mean(e, axis=1, keepdims=True) - n * jnp.mean(e * n, axis=1, keepdims=True)
    ) * inv_std
    hidden_grad = (up + back).astype(BF)
    hg_ref[0] = hidden_grad
    wo_acc[...] += mm(hidden_grad, attended_low, 0, 0)
    wp_acc[...] += mm(hidden_grad, pooled, 0, 0)
    misc_acc[0:1, :] += jnp.sum(before_grad.astype(F32), axis=0, keepdims=True)
    misc_acc[1:2, :D_OUT] += jnp.sum(second_grad * n, axis=0, keepdims=True)
    misc_acc[2:3, :D_OUT] += jnp.sum(second_grad, axis=0, keepdims=True)
    misc_acc[3:4, :D_OUT] += jnp.sum(up, axis=0, keepdims=True)
    misc_acc[4:5, :D_OUT] += jnp.sum(hidden_grad.astype(F32), axis=0, keepdims=True)
    attended_grad = mm(hidden_grad, wo_ref[...], 1, 1).astype(BF).astype(F32)
    lane = iota((queries, LANES), 1)
    eye = jnp.where(iota((HEAD_DIM, LANES), 0) == iota((HEAD_DIM, LANES), 1), 1.0, 0.0).astype(BF)
    fill = jnp.zeros((queries, LANES - HEAD_DIM), F32)
    for h in range(HEADS):
        own = attended_grad[:, HEAD_DIM * h : HEAD_DIM * (h + 1)]
        for factor, do_ref, dot_ref in zip(
            factors[h], (do1_ref, do2_ref), (do1t_ref, do2t_ref), strict=True
        ):
            scaled = (own * factor).astype(BF).astype(F32)
            inner = jnp.sum(scaled * heads[h], axis=1, keepdims=True)
            high = inner.astype(BF).astype(F32)
            grad = jnp.concatenate([scaled, fill], axis=1)
            grad = jnp.where(lane == HEAD_DIM, -high, grad)
            grad = jnp.where(lane == HEAD_DIM + 1, high - inner, grad).astype(BF)
            do_ref[0, h] = grad
            dot_ref[0, h] = mm(eye, grad, 1, 1).astype(BF)

    if step == clips - 1:
        me = me_ref[0]
        wpt_ref[...] = wp_acc[...]
        for u in range(4):
            for k in range(4):
                misc_acc[8 + u : 9 + u, HEAD_DIM * k : HEAD_DIM * (k + 1)] = misc_acc[
                    1 + k : 2 + k, HEAD_DIM * u : HEAD_DIM * (u + 1)
                ]
        for r in range(4):
            u = me ^ r
            ref, at = (send_ref if r & 1 else keep_ref), r >> 1
            wide = pl.ds(pl.multiple_of(u * 384, LANES), 384)
            tall = pl.ds(pl.multiple_of(u * 96, 8), 96)
            ref[at, 0:384, :] = we_acc[:, wide].astype(BF)
            ref[at, 384:768, :] = ws_acc[:, wide].astype(BF)
            ref[at, 768:864, :] = wo_acc[tall, :].astype(BF)
            wp = wp_acc[tall, :]
            ref[at, 864:912, :] = jnp.concatenate([wp[:48, :D_IN], wp[48:, :D_IN]], axis=1).astype(BF)
            bias = misc_acc[0:1, wide]
            others = misc_acc[pl.ds(8 + u, 1), :384]
            row = iota((48, 384), 0)
            ref[at, 912:960, :] = jnp.where(row == 0, bias, jnp.where(row == 1, others, 0.0)).astype(BF)


def middle(me, o1, o2, pooled, up, table, wp, wo, we, ws):
    clips = len(pooled)
    queries = pooled[0].shape[0]
    grad = (clips, HEADS, queries, LANES)
    grad_t = (clips, HEADS, HEAD_DIM, queries)
    return call(
        functools.partial(middle_body, clips),
        (clips,),
        [
            (pl.BlockSpec(memory_space=pltpu.SMEM), me),
            *(whole(value) for value in o1 + o2 + pooled),
            part(up),
            whole(table),
            whole(wp),
            whole(wo),
            whole(we),
            whole(ws),
        ],
        [
            out_part((clips, queries, D_OUT), F32),
            out_part((clips, queries, D_OUT), BF),
            out_part(grad, BF),
            out_part(grad, BF),
            out_part(grad_t, BF),
            out_part(grad_t, BF),
            out_whole((2, 960, 384), BF),
            out_whole((2, 960, 384), BF),
            out_whole((D_OUT, 2 * LANES), F32),
        ],
        [
            pltpu.VMEM((D_OUT, FF), F32),
            pltpu.VMEM((D_OUT, FF), F32),
            pltpu.VMEM((D_OUT, D_OUT), F32),
            pltpu.VMEM((D_OUT, 2 * LANES), F32),
            pltpu.VMEM((16, FF), F32),
        ],
        name="middle",
        cost=24,
    )


def backward_body(
    na_ref,
    nb_ref,
    wt_ref,
    p_ref,
    kt_ref,
    vt_ref,
    do_ref,
    dot_ref,
    qt_ref,
    dq_ref,
    dw_ref,
    ga_ref,
    gb_ref,
    n_ref,
    g_ref,
):
    rows = na_ref.shape[1]
    h = pl.program_id(0)

    @pl.when(h == 0)
    def _():
        n_ref[:, :rows] = na_ref[...]
        n_ref[:, rows:] = nb_ref[...]

    p = p_ref[0]
    kt = kt_ref[0]
    dp = mm(do_ref[0], vt_ref[0], 1, 0)
    ds = p * dp.astype(BF)
    dq_ref[0] = mm(ds, kt, 1, 1)
    both = jnp.concatenate([mm(qt_ref[0], ds, 1, 0), mm(dot_ref[0], p, 1, 0)], axis=0).astype(BF)
    dw_ref[0] = jnp.concatenate(
        [mm(both, n_ref[...], 1, 1), jnp.zeros((2 * HEAD_DIM, 2 * LANES - EXT), F32)], axis=1
    )
    w = jnp.concatenate(
        [wt_ref[HEADS + h][:HEAD_DIM, :D_IN], wt_ref[2 * HEADS + h][:HEAD_DIM, :D_IN]], axis=0
    )
    g = mm(w, both, 0, 0)

    @pl.when(h == 0)
    def _():
        g_ref[...] = g

    @pl.when((h > 0) & (h < HEADS - 1))
    def _():
        g_ref[...] += g

    @pl.when(h == HEADS - 1)
    def _():
        total = (g_ref[...] + g).astype(BF)
        ga_ref[...] = total[:, :rows]
        gb_ref[...] = total[:, rows:]


def backward(clip, na, nb, wt, p, kt, vt, do, dot, qt, after=()):
    rows = na.shape[1]
    queries = qt.shape[2]
    return call(
        backward_body,
        (HEADS,),
        [
            whole(na),
            whole(nb),
            whole(wt),
            part(p),
            part(kt),
            part(vt),
            at_head(do, clip),
            at_head(dot, clip),
            part(qt),
        ],
        [
            out_part((HEADS, queries, LANES), F32),
            out_part((HEADS, 2 * HEAD_DIM, 2 * LANES), F32),
            out_whole((D_IN, rows), BF),
            out_whole((D_IN, rows), BF),
        ],
        [pltpu.VMEM((EXT, 2 * rows), BF), pltpu.VMEM((D_IN, 2 * rows), F32)],
        name="attend_back",
        after=after,
        cost=18,
    )


def gather_body(clips, me_ref, *refs):
    dq_refs, dw_refs, pooled_refs = (
        refs[: 2 * clips],
        refs[2 * clips : 4 * clips],
        refs[4 * clips : 5 * clips],
    )
    hg_ref, wt_ref, wpt_ref, table_ref = refs[5 * clips : 5 * clips + 4]
    g_ref, keep_ref, send_ref, dw_acc, line_ref, shard_ref = refs[5 * clips + 4 :]
    gain_sum = jnp.zeros((1, D_IN), F32)
    shift_sum = jnp.zeros((1, D_IN), F32)
    low = [[None] * HEADS for _ in range(clips)]
    for h in range(HEADS):
        columns = slice(HEAD_DIM * h, HEAD_DIM * (h + 1))
        dw = jnp.zeros((LANES, 2 * LANES), F32)
        bias = jnp.zeros((1, LANES), F32)
        for c in range(clips):
            dq = (dq_refs[2 * c][h] + dq_refs[2 * c + 1][h]) * SCALE
            bias = bias + jnp.sum(dq, axis=0, keepdims=True)
            low[c][h] = dq.astype(BF)
            dw = dw + mm(low[c][h], pooled_refs[c][...], 0, 0)
        dw_acc[h] = dw[:HEAD_DIM]
        line_ref[0:1, columns] = bias[:, :HEAD_DIM]
        total = dw_refs[0][h]
        for ref in dw_refs[1:]:
            total = total + ref[h]
        dw_acc[HEADS + h] = total[:HEAD_DIM]
        dw_acc[2 * HEADS + h] = total[HEAD_DIM:]
        sums = jnp.concatenate(
            [total[HEAD_DIM:, LANES:], jnp.zeros((LANES - HEAD_DIM, LANES), F32)], axis=0
        ).T
        line_ref[1:2, columns] = sums[D_IN - LANES : D_IN - LANES + 1, :HEAD_DIM]
    wp = wt_ref[3 * HEADS :].reshape(D_OUT, 2 * LANES)[:, :D_IN]
    for c in range(clips):
        g = mm(hg_ref[c], wp, 1, 0)
        for h in range(HEADS):
            g = g + mm(low[c][h], wt_ref[h][:, :D_IN], 1, 0)
        g_ref[c] = g
    terms = [(wt_ref[b][:HEAD_DIM, :D_IN], dw_acc[b]) for b in range(3 * HEADS)]
    for w, dw in [*terms, (wp, wpt_ref[...])]:
        w = w.astype(F32)
        gain_sum = gain_sum + jnp.sum(w * dw[:, :D_IN], axis=0, keepdims=True)
        shift_sum = shift_sum + jnp.sum(w * dw[:, D_IN : D_IN + 1], axis=0, keepdims=True)
    gain_sum = (gain_sum - vec(table_ref, V_SHIFT1, D_IN) * shift_sum) / vec(
        table_ref, V_GAIN1, D_IN
    )
    line_ref[2:3, :D_IN] = gain_sum
    line_ref[3:4, :D_IN] = shift_sum
    for u in range(4):
        at = 0
        for source, size in ((0, 96), (1, 96), (2, 48), (3, 48)):
            shard_ref[u : u + 1, at : at + size] = line_ref[
                source : source + 1, size * u : size * (u + 1)
            ]
            at += size
        shard_ref[u : u + 1, at:] = jnp.zeros((1, D_OUT - at), F32)
    for r in range(4):
        u = me_ref[0] ^ r
        ref, at = (send_ref if r & 1 else keep_ref), r >> 1
        rows = jnp.concatenate([dw_acc[3 * u + i][:, :D_IN] for i in range(3)], axis=0)
        ref[at, :144, :] = jnp.concatenate([rows[:144], rows[144:]], axis=1).astype(BF)
        ref[at, 144:, :] = jnp.where(
            iota((16, D_OUT), 0) == 0, shard_ref[pl.ds(u, 1), :], 0.0
        ).astype(BF)


def gather(me, dq, dw, pooled, hg, wt, wpt, table, after=()):
    clips, queries, _ = hg.shape
    return call(
        functools.partial(gather_body, clips),
        (1,),
        [
            (pl.BlockSpec(memory_space=pltpu.SMEM), me),
            *(whole(value) for value in (*dq, *dw, *pooled, hg, wt, wpt, table)),
        ],
        [
            out_whole((clips, queries, D_IN), F32),
            out_whole((2, 160, D_OUT), BF),
            out_whole((2, 160, D_OUT), BF),
        ],
        [
            pltpu.VMEM((3 * HEADS, HEAD_DIM, 2 * LANES), F32),
            pltpu.VMEM((8, D_OUT), F32),
            pltpu.VMEM((8, D_OUT), F32),
        ],
        name="gather",
        after=after,
        cost=6,
    )


def final_body(clips, terms, tok_ref, *refs):
    part_refs = refs[: clips * terms]
    g_ref, cols_ref, out_ref, total_ref = refs[clips * terms :]
    slots, _, units = tok_ref.shape[1:]
    for c in range(clips):

        @pl.when(pl.program_id(0) == c)
        def _():
            total = part_refs[terms * c][...].astype(F32)
            for ref in part_refs[terms * c + 1 : terms * (c + 1)]:
                total = total + ref[...].astype(F32)
            total_ref[...] = total

    gain = cols_ref[:, 0:1]
    spread = g_ref[0].T * 0.25
    for s in range(slots):
        p = 2 * (s >> 3) + ((s >> 1) & 1)
        grad = total_ref[:, units * s : units * (s + 1)] + spread[:, units * p : units * (p + 1)]
        x = tok_ref[0, s].astype(F32)
        center = x - jnp.mean(x, axis=0, keepdims=True)
        inv_std = lax.rsqrt(jnp.mean(center * center, axis=0, keepdims=True) + 1e-06)
        n = center * inv_std
        e = grad * gain
        out_ref[0, s] = (
            e - jnp.mean(e, axis=0, keepdims=True) - n * jnp.mean(e * n, axis=0, keepdims=True)
        ) * inv_std


def final(tokens, parts, g, cols):
    clips, slots, _, units = tokens.shape
    terms = len(parts[0])
    return call(
        functools.partial(final_body, clips, terms),
        (clips,),
        [
            part(tokens),
            *(whole(value) for values in parts for value in values),
            part(g),
            whole(cols),
        ],
        [out_part(tokens.shape, F32)],
        [pltpu.VMEM((D_IN, slots * units), F32)],
        name="final",
        cost=7,
    )[0]


def swap_unit(value, bit):
    return lax.ppermute(value, "unit", [(i, i ^ bit) for i in range(4)])


def swap_clip(value, bit):
    size = lax.axis_size("clip")
    return lax.ppermute(value, "clip", [(i, i ^ bit) for i in range(size)])


def add(a, b):
    return (a.astype(F32) + b.astype(F32)).astype(BF)


def halve(value, bit):
    upper = (lax.axis_index("clip") & bit) != 0
    half = value.shape[0] // 2
    mine = jnp.where(upper, value[half:], value[:half])
    other = jnp.where(upper, value[:half], value[half:])
    return add(mine, swap_clip(other, bit))


def double(value, bit):
    upper = (lax.axis_index("clip") & bit) != 0
    other = swap_clip(value, bit)
    return jnp.where(upper, jnp.concatenate([other, value]), jnp.concatenate([value, other]))


def clip_bits(rows):
    size, bit, cut, rest = lax.axis_size("clip"), 1, [], []
    while bit < size:
        if not rest and rows % 16 == 0:
            cut.append(bit)
            rows //= 2
        else:
            rest.append(bit)
        bit *= 2
    return cut, rest


def reduce_clips(value):
    cut, rest = clip_bits(value.shape[0])
    for bit in cut:
        value = halve(value, bit)
    for bit in rest:
        value = add(value, swap_clip(value, bit))
    for bit in reversed(cut):
        value = double(value, bit)
    return value


def shards(
    tokens,
    first_gain,
    first_shift,
    proj_weight,
    proj_bias,
    qkv_weight,
    query_bias,
    value_bias,
    output_weight,
    output_bias,
    second_gain,
    second_shift,
    expand_weight,
    expand_bias,
    shrink_weight,
    shrink_bias,
    frame_counts,
    unit_frames,
    cotangent,
):
    clips, units = tokens.shape[:2]
    me = lax.axis_index("unit").astype(jnp.int32).reshape(1)
    lines = [
        [first_gain],
        [first_shift],
        [proj_bias],
        [output_bias],
        [second_gain],
        [second_shift],
        [shrink_bias],
        [expand_bias],
        [query_bias, jnp.zeros_like(query_bias), value_bias],
    ]
    pieces = []
    for line in lines:
        pieces += line
        pieces.append(jnp.zeros((FF - sum(v.shape[0] for v in line),), BF))
    table = jnp.concatenate(pieces).astype(F32).reshape(len(lines), FF)
    cols = jnp.stack([first_gain, first_shift], axis=1).astype(F32)
    invalid = (unit_frames >= frame_counts[:, None]).astype(F32).reshape(clips, 1, units)
    flat = tokens.transpose(0, 2, 3, 1)
    upstream = cotangent.transpose(0, 2, 1, 3).reshape(clips, 4 * units, D_OUT)
    near, across, pooled = [], [], []
    for c in range(clips):
        n, pool = normed_tokens(c, flat, invalid, cols)
        near.append((n, swap_unit(n, 1)))
        across.append(swap_unit(n, 2))
        pooled.append(pool)
    wt, query = queries_of(qkv_weight, proj_weight, table, pooled)
    own, rest, far = [], [], []
    for c in range(clips):
        own.append(forward(*near[c], wt, query[c][0], after=[v[3] for v in own[-1:]]))
    for c in range(clips):
        held, _ = lax.optimization_barrier((across[c], own[0][3]))
        far.append((held, swap_unit(held, 1)))
        rest.append(
            forward(*far[c], wt, query[c][0], after=[v[3] for v in (own + rest)[-1:]])
        )
    out, hg, do1, do2, do1t, do2t, keep, send, wpt = middle(
        me,
        [value[3] for value in own],
        [value[3] for value in rest],
        pooled,
        upstream,
        table,
        proj_weight,
        output_weight,
        expand_weight,
        shrink_weight,
    )
    dq, dw = [[None, None] for _ in range(clips)], [[None, None] for _ in range(clips)]
    parts = [[] for _ in range(clips)]
    first = add(keep, swap_unit(send, 1))
    after = []
    for c in range(clips):
        dq[c][1], dw[c][1], ga, gb = backward(
            c, *far[c], wt, *rest[c][:3], do2, do2t, query[c][1], after=after
        )
        parts[c].append(add(ga, swap_unit(gb, 1)))
        after = [dq[c][1], first]
        if c == 0:
            first = add(first[0], swap_unit(first[1], 2))
    cut, left = clip_bits(first.shape[0])
    for c in range(clips):
        after += [parts[c][0]]
        dq[c][0], dw[c][0], ga, gb = backward(
            c, *near[c], wt, *own[c][:3], do1, do1t, query[c][1], after=after
        )
        parts[c][0] = swap_unit(parts[c][0], 2)
        parts[c] += [ga, swap_unit(gb, 1)]
        if cut:
            first = halve(first, cut[0])
            cut = cut[1:]
        after = [dq[c][0], first, parts[c][0]]
    done = clip_bits(960)[0]
    for bit in cut:
        first = halve(first, bit)
    for bit in left:
        first = add(first, swap_clip(first, bit))
    for bit in reversed(done):
        first = double(first, bit)
    g, keep, send = gather(
        me, [v for pair in dq for v in pair], [v for pair in dw for v in pair], pooled, hg, wt, wpt, table,
        after=after,
    )
    second = add(keep, swap_unit(send, 1))
    second = add(second[0], swap_unit(second[1], 2))
    second = reduce_clips(second).astype(F32)
    first = first.astype(F32)
    input_grad = final(flat, parts, g, cols)

    def lanes(value, row, start, size):
        return value[row, start : start + size]

    proj = jnp.concatenate([first[864:912, :D_IN], first[864:912, D_IN:]], axis=0)
    qkv = jnp.concatenate([second[:144, :D_IN], second[:144, D_IN:]], axis=0)
    return (
        out.reshape(clips, 4, units, D_OUT).transpose(0, 2, 1, 3),
        input_grad.transpose(0, 3, 1, 2),
        lanes(second, 144, 192, 48),
        lanes(second, 144, 240, 48),
        proj.T,
        lanes(first, 913, 288, 96),
        qkv.T,
        lanes(second, 144, 0, 96),
        lanes(second, 144, 96, 96),
        first[768:864].T,
        lanes(first, 913, 288, 96),
        lanes(first, 913, 0, 96),
        lanes(first, 913, 96, 96),
        first[:384],
        lanes(first, 912, 0, 384),
        first[384:768].T,
        lanes(first, 913, 192, 96),
    )


def solution(mesh):
    every = P()
    split = P("clip", "unit", None, None)
    return jax.shard_map(
        shards,
        mesh=mesh,
        in_specs=(split,) + (every,) * 15 + (P("clip"), P("clip", "unit"), split),
        out_specs=(
            split,
            split,
            P("unit"),
            P("unit"),
            P(None, "unit"),
            P("unit"),
            P(None, "unit"),
            P("unit"),
            P("unit"),
            P(None, "unit"),
            P("unit"),
            P("unit"),
            P("unit"),
            P(None, "unit"),
            P("unit"),
            P("unit", None),
            P("unit"),
        ),
        check_vma=False,
    )
```

time: 971 us -> 284 us (0.29)
  matrix products: 289 us -> 0 us
  local copies, waits for them, and re-layouts: 233 us -> 18.4 us
  Pallas kernels: 0 us -> 194 us
  other arithmetic: 151 us -> 8.61 us
  waiting for transfers between devices: 167 us -> 31.7 us
  blocking collectives: 103 us -> 0 us
  starting transfers between devices: 0.58 us -> 25.4 us
  between operations: 17.1 us -> 1.45 us
    dot_general x29 -> x0, matrix products: 289 us -> none  [the longest x4 62.4 us: clip_scores(): jnp.einsum('qhd,khd->hqk', query_one, key_heads, preferred_element_type=j...]
    pallas_call x0 -> x14, Pallas kernels: none -> 194 us  [call(): pl.pallas_call(run, grid=grid, in_specs=[spec for spec, _ in ins], out_sp...]
    reduce_scatter x4 -> x0, waiting for transfers between devices: 135 us -> none  [the longest x1 82.5 us: shards(): lax.psum_scatter(value_grad_all.astype(jnp.bfloat16), 'unit', scatter_dim...]
    psum x1 -> x0, blocking collectives: 86.1 us -> none  [shards(): lax.psum((shares[0], shares[1], shares[2], shares[3], shares[4], shares[5...]
    convert_element_type x20 -> x15, other arithmetic: 73.5 us -> 6.97 us  [the longest x12 6.11 us: add(): return (a.astype(F32) + b.astype(F32)).astype(BF)]
    reduce_sum x14 -> x0, other arithmetic: 65.6 us -> none  [the longest x2 35.5 us: attend(): denominator = jnp.sum(weights, axis=-1, keepdims=True)]
    while x20 -> x0, local copies, waits for them, and re-layouts: 53.2 us -> none  [the longest x3 52.6 us: shards(): lax.map(attend, (query_heads, key_rows, value_rows, key_valid))]
    dynamic_update_slice x12 -> x0, local copies, waits for them, and re-layouts: 51.4 us -> none  [the longest x6 47.6 us: shards(): lax.map(attend_back, (query_heads, key_rows, value_rows, key_valid, log_t...]
  transfers between devices with their start and end apart: 9 -> 27, of which waited for: 3 -> 9; matrix products, arithmetic and copies ran while one was open for 47% -> 4% of each run, Pallas kernels for 0% -> 52%
where the time goes in v1:
time: 284 us; the launch traced here: 279 us
  Pallas kernels  194 us (68%)
  waiting for transfers between devices  31.7 us (11%)
  starting transfers between devices  25.4 us (9%)
  local copies, waits for them, and re-layouts  18.4 us (6%)
  other arithmetic  8.61 us (3%)
    pallas_call x14, Pallas kernels, call(): pl.pallas_call(run, grid=grid, in_specs=[spec for spec, _ in ins], out_sp...  194 us
    ppermute x16, waiting for transfers between devices, swap_unit(): return lax.ppermute(value, 'unit', [(i, i ^ bit) for i in range(4)])  22.1 us
    ppermute x11, starting transfers between devices, swap_clip(): return lax.ppermute(value, 'clip', [(i, i ^ bit) for i in range(size)])  14.5 us
    ppermute x16, starting transfers between devices, swap_unit(): return lax.ppermute(value, 'unit', [(i, i ^ bit) for i in range(4)])  10.9 us
    unnamed x71, local copies, waits for them, and re-layouts  9.92 us
    ppermute x11, waiting for transfers between devices, swap_clip(): return lax.ppermute(value, 'clip', [(i, i ^ bit) for i in range(size)])  9.63 us
    convert_element_type x12, other arithmetic, add(): return (a.astype(F32) + b.astype(F32)).astype(BF)  6.11 us
  transfers between devices with their start and end apart: 27, of which 9 were waited for; matrix products, arithmetic and copies ran while one was open for 4% of the time, Pallas kernels for 52%

profile of v1, /device:TPU:0, one launch (start us, length us, event | category | flops | bytes accessed | tf_op | source)
XLA Modules:
  0.0 279.4 jit_solution(4269434069638091149)
XLA Ops:
  4.1 3.1 %normed.2 = (bf16[208,1568]{1,0:T(8,128)(2,1)}, bf16[392,256]{1,0:T(8,128)(2,1)}) custom-call(bf16[2,16,192,98]{3,2,1,0:T(8,128)(2,1)} %bitcast.52, f32[2,1,98]{2,1,0:T(1,128)} %bitcast.50, f32[192,2]{1,0:T(8,128)} %convert_element_type.131.refs_2_.refs_8_), custom_call_target="tpu_custom_call" | custom-call | flops 3300000000 | bytes 3000000 | tf_op jit(solution)/shard_map/normed/pallas_call | solution.py:39
  7.8 2.6 collective-permute-start.2
  10.4 3.1 %normed.3 = (bf16[208,1568]{1,0:T(8,128)(2,1)}, bf16[392,256]{1,0:T(8,128)(2,1)}) custom-call(bf16[2,16,192,98]{3,2,1,0:T(8,128)(2,1)} %bitcast.53, f32[2,1,98]{2,1,0:T(1,128)} %bitcast.51, f32[192,2]{1,0:T(8,128)} %convert_element_type.131.refs_2_.refs_8_), custom_call_target="tpu_custom_call" | custom-call | flops 3300000000 | bytes 3000000 | tf_op jit(solution)/shard_map/normed/pallas_call | solution.py:39
  16.2 3.6 %queries.1 = (bf16[15,128,256]{2,1,0:T(8,128)(2,1)}, bf16[4,392,128]{2,1,0:T(8,128)(2,1)}, bf16[4,96,392]{2,1,0:T(8,128)(2,1)}, bf16[4,392,128]{2,1,0:T(8,128)(2,1)}, bf16[4,96,392]{2,1,0:T(8,128)(2,1)}) custom-call(bf16[192,1152]{1,0:T(8,128)(2,1)} %refs_0_.1, bf16[192,384]{1,0:T(8,128)(2,1)} %refs_9_.1, f32[9,1536]{1,0:T(8,128)} %reshape.64.refs_2_.refs_8_.refs_14_, ...), custom_call_target="tpu_custom_call" | custom-call | flops 5500000256 | bytes 5000000 | tf_op jit(solution)/shard_map/queries/pallas_call | solution.py:39
  20.7 16.8 %attend.4 = (bf16[4,392,3136]{2,1,0:T(8,128)(2,1)}, bf16[4,128,3136]{2,1,0:T(8,128)(2,1)}, bf16[4,128,3136]{2,1,0:T(8,128)(2,1)}, f32[4,392,128]{2,1,0:T(8,128)}) custom-call(bf16[208,1568]{1,0:T(8,128)(2,1)} %get-tuple-element.72.refs_0_, bf16[208,1568]{1,0:T(8,128)(2,1)} %copy-done.23, bf16[15,128,256]{2,1,0:T(8,128)(2,1)} %get-tuple-element.75.refs_2_.refs_12_, ...), custom_call_target="tpu_custom_call" | custom-call | flops 17600000000 | bytes 16000000 | tf_op jit(solution)/shard_map/attend/pallas_call | solution.py:39
  37.7 3.8 %collective-permute-done.4.refs_0_ = bf16[208,1568]{1,0:T(8,128)(2,1)S(1)} collective-permute-done((bf16[208,1568]{1,0:T(8,128)(2,1)}, bf16[208,1568]{1,0:T(8,128)(2,1)S(1)}, u32[]{:S(2)}, u32[]{:S(2)}) %collective-permute-start.4) | collective-permute-done | bytes 652320 | tf_op jit(solution)/shard_map/ppermute | solution.py:624
  42.4 16.7 %attend.5 = (bf16[4,392,3136]{2,1,0:T(8,128)(2,1)}, bf16[4,128,3136]{2,1,0:T(8,128)(2,1)}, bf16[4,128,3136]{2,1,0:T(8,128)(2,1)}, f32[4,392,128]{2,1,0:T(8,128)}) custom-call(bf16[208,1568]{1,0:T(8,128)(2,1)} %get-tuple-element.78.refs_0_, bf16[208,1568]{1,0:T(8,128)(2,1)} %copy-done.22, bf16[15,128,256]{2,1,0:T(8,128)(2,1)} %get-tuple-element.75.refs_2_.refs_12_, ...), custom_call_target="tpu_custom_call" | custom-call | flops 17600000000 | bytes 16000000 | tf_op jit(solution)/shard_map/attend/pallas_call | solution.py:39
  60.0 16.6 %attend.6 = (bf16[4,392,3136]{2,1,0:T(8,128)(2,1)}, bf16[4,128,3136]{2,1,0:T(8,128)(2,1)}, bf16[4,128,3136]{2,1,0:T(8,128)(2,1)}, f32[4,392,128]{2,1,0:T(8,128)}) custom-call(bf16[208,1568]{1,0:T(8,128)(2,1)} %copy-done.25, bf16[208,1568]{1,0:T(8,128)(2,1)} %copy-done.27, bf16[15,128,256]{2,1,0:T(8,128)(2,1)} %get-tuple-element.75.refs_2_.refs_12_, ...), custom_call_target="tpu_custom_call" | custom-call | flops 17600000000 | bytes 16000000 | tf_op jit(solution)/shard_map/attend/pallas_call | solution.py:39
  77.5 16.7 %attend.7 = (bf16[4,392,3136]{2,1,0:T(8,128)(2,1)}, bf16[4,128,3136]{2,1,0:T(8,128)(2,1)}, bf16[4,128,3136]{2,1,0:T(8,128)(2,1)}, f32[4,392,128]{2,1,0:T(8,128)}) custom-call(bf16[208,1568]{1,0:T(8,128)(2,1)} %copy-done.24, bf16[208,1568]{1,0:T(8,128)(2,1)} %copy-done.26, bf16[15,128,256]{2,1,0:T(8,128)(2,1)} %get-tuple-element.75.refs_2_.refs_12_, ...), custom_call_target="tpu_custom_call" | custom-call | flops 17600000000 | bytes 16000000 | tf_op jit(solution)/shard_map/attend/pallas_call | solution.py:39
  94.2 24.3 %middle.1 = (f32[2,392,384]{2,1,0:T(8,128)}, bf16[2,392,384]{2,1,0:T(8,128)(2,1)}, bf16[2,4,392,128]{3,2,1,0:T(8,128)(2,1)}, bf16[2,4,392,128]{3,2,1,0:T(8,128)(...) custom-call(s32[1]{0:T(128)} %bitcast.refs_0_, ...), custom_call_target="tpu_custom_call" | custom-call | flops 26400000000 | bytes 24000000 | tf_op jit(solution)/shard_map/middle/pallas_call | solution.py:39
  119.0 18.0 %attend_back.4 = (f32[4,392,128]{2,1,0:T(8,128)}, f32[4,192,256]{2,1,0:T(8,128)}, bf16[192,1568]{1,0:T(8,128)(2,1)}, bf16[192,1568]{1,0:T(8,128)(2,1)}) custom-call(bf16[208,1568]{1,0:T(8,128)(2,1)} %copy-done.25, bf16[208,1568]{1,0:T(8,128)(2,1)} %copy-done.27, bf16[15,128,256]{2,1,0:T(8,128)(2,1)} %get-tuple-element.75.refs_2_.refs_12_, ...), custom_call_target="tpu_custom_call" | custom-call | flops 19800000512 | bytes 18000000 | tf_op jit(solution)/shard_map/attend_back/pallas_call | solution.py:39
  137.1 1.5 add_convert_fusion.refs_10_
  138.6 18.1 %attend_back.5 = (f32[4,392,128]{2,1,0:T(8,128)}, f32[4,192,256]{2,1,0:T(8,128)}, bf16[192,1568]{1,0:T(8,128)(2,1)}, bf16[192,1568]{1,0:T(8,128)(2,1)}) custom-call(bf16[208,1568]{1,0:T(8,128)(2,1)} %copy-done.24, bf16[208,1568]{1,0:T(8,128)(2,1)} %copy-done.26, bf16[15,128,256]{2,1,0:T(8,128)(2,1)} %get-tuple-element.75.refs_2_.refs_12_, ...), custom_call_target="tpu_custom_call" | custom-call | flops 19800000512 | bytes 18000000 | tf_op jit(solution)/shard_map/attend_back/pallas_call | solution.py:39
  157.3 1.8 collective-permute-start.9
  160.0 1.7 collective-permute-start.12
  161.6 15.1 %collective-permute-done.9 = bf16[960,384]{1,0:T(8,128)(2,1)S(1)} collective-permute-done((bf16[960,384]{1,0:T(8,128)(2,1)S(1)}, bf16[960,384]{1,0:T(8,128)(2,1)S(1)}, u32[]{:S(2)}, u32[]{:S(2)}) %collective-permute-start.9) | collective-permute-done | bytes 737312 | tf_op jit(solution)/shard_map/ppermute | solution.py:624
  177.0 1.9 collective-permute-start.13
  178.9 18.1 %attend_back.6 = (f32[4,392,128]{2,1,0:T(8,128)}, f32[4,192,256]{2,1,0:T(8,128)}, bf16[192,1568]{1,0:T(8,128)(2,1)}, bf16[192,1568]{1,0:T(8,128)(2,1)}) custom-call(bf16[208,1568]{1,0:T(8,128)(2,1)} %get-tuple-element.72.refs_0_, bf16[208,1568]{1,0:T(8,128)(2,1)} %copy-done.23, bf16[15,128,256]{2,1,0:T(8,128)(2,1)} %get-tuple-element.75.refs_2_.refs_12_, ...), custom_call_target="tpu_custom_call" | custom-call | flops 19800000512 | bytes 18000000 | tf_op jit(solution)/shard_map/attend_back/pallas_call | solution.py:39
  198.3 1.6 collective-permute-start.15
  200.8 17.9 %attend_back.7 = (f32[4,392,128]{2,1,0:T(8,128)}, f32[4,192,256]{2,1,0:T(8,128)}, bf16[192,1568]{1,0:T(8,128)(2,1)}, bf16[192,1568]{1,0:T(8,128)(2,1)}) custom-call(bf16[208,1568]{1,0:T(8,128)(2,1)} %get-tuple-element.78.refs_0_, bf16[208,1568]{1,0:T(8,128)(2,1)} %copy-done.22, bf16[15,128,256]{2,1,0:T(8,128)(2,1)} %get-tuple-element.75.refs_2_.refs_12_, ...), custom_call_target="tpu_custom_call" | custom-call | flops 19800000512 | bytes 18000000 | tf_op jit(solution)/shard_map/attend_back/pallas_call | solution.py:39
  218.7 1.8 add_convert_fusion.5.refs_16_
  220.5 5.8 %gather.1 = (f32[2,392,192]{2,1,0:T(8,128)}, bf16[2,160,384]{2,1,0:T(8,128)(2,1)}, bf16[2,160,384]{2,1,0:T(8,128)(2,1)}) custom-call(s32[1]{0:T(128)} %bitcast.refs_0_, f32[4,392,128]{2,1,0:T(8,128)} %get-tuple-element.114.refs_9_.refs_1_, f32[4,392,128]{2,1,0:T(8,128)} %get-tuple-element.103.refs_9_.refs_2_, ...), custom_call_target="tpu_custom_call" | custom-call | flops 6600000000 | bytes 6000000 | tf_op jit(solution)/shard_map/gather/pallas_call | solution.py:39
  226.3 1.7 collective-permute-done.16
  229.1 1.5 collective-permute-start.17
  233.1 1.4 collective-permute-done.17
  235.4 2.7 collective-permute-start.23
  239.4 2.4 collective-permute-done.23
  241.8 1.8 collective-permute-start.24
  243.7 2.1 collective-permute-start.20
  245.7 1.8 collective-permute-done.24
  249.7 3.4 %collective-permute-done.25 = bf16[240,384]{1,0:T(8,128)(2,1)S(1)} collective-permute-done((bf16[240,384]{1,0:T(8,128)(2,1)S(1)}, bf16[240,384]{1,0:T(8,128)(2,1)S(1)}, u32[]{:S(2)}, u32[]{:S(2)}) %collective-permute-start.25) | collective-permute-done | bytes 184352 | tf_op jit(solution)/shard_map/ppermute | solution.py:629
  256.5 15.1 %final.1 = f32[2,16,192,98]{3,2,1,0:T(8,128)} custom-call(bf16[2,16,192,98]{3,2,1,0:T(8,128)(2,1)} %bitcast.54, bf16[192,1568]{1,0:T(8,128)(2,1)} %copy-done.28, bf16[192,1568]{1,0:T(8,128)(2,1)} %get-tuple-element.107.refs_2_, bf16[192,1568]{1,0:T(8,128)(2,1)} %copy-done.31, bf16[192,1568]{1,0:T(8,128)(2,1)} %collective-permute-done.12.refs_17_.refs_4_, ...), custom_call_target="tpu_custom_call" | custom-call | flops 7699999744 | bytes 7000000 | tf_op jit(solution)/shard_map/final/pallas_call | solution.py:39
  (155 shorter events, 33.6 us)
Async XLA Ops:
  7.3 12.6 %collective-permute-start = (bf16[208,1568]{1,0:T(8,128)(2,1)}, bf16[208,1568]{1,0:T(8,128)(2,1)S(1)}, u32[]{:S(2)}, u32[]{:S(2)}) collective-permute-start(bf16[208,1568]{1,0:T(8,128)(2,1)} %get-tuple-element.72.refs_0_), channel_id=1, source_target_pairs={{0,1},{1,0},{2,3},{3,2},{4,5},{5,4},{6,7},{7,6},{8,9},{9,8},{10,11... | collective-permute-start | bytes 1956872 | tf_op jit(solution)/shard_map/ppermute | solution.py:624
  7.8 29.7 %collective-permute-start.2 = (bf16[208,1568]{1,0:T(8,128)(2,1)}, bf16[208,1568]{1,0:T(8,128)(2,1)S(1)}, u32[]{:S(2)}, u32[]{:S(2)}) collective-permute-start(bf16[208,1568]{1,0:T(8,128)(2,1)} %get-tuple-element.72.refs_0_), channel_id=1, source_target_pairs={{0,2},{1,3},{2,0},{3,1},{4,6},{5,7},{6,4},{7,5},{8,10},{9,11},{10,... | collective-permute-start | bytes 1956872 | tf_op jit(solution)/shard_map/ppermute | solution.py:624
  13.5 28.0 %collective-permute-start.1 = (bf16[208,1568]{1,0:T(8,128)(2,1)}, bf16[208,1568]{1,0:T(8,128)(2,1)S(1)}, u32[]{:S(2)}, u32[]{:S(2)}) collective-permute-start(bf16[208,1568]{1,0:T(8,128)(2,1)} %get-tuple-element.78.refs_0_), channel_id=1, source_target_pairs={{0,1},{1,0},{2,3},{3,2},{4,5},{5,4},{6,7},{7,6},{8,9},{9,8},{10,11... | collective-permute-start | bytes 1956872 | tf_op jit(solution)/shard_map/ppermute | solution.py:624
  13.7 27.9 %collective-permute-start.4 = (bf16[208,1568]{1,0:T(8,128)(2,1)}, bf16[208,1568]{1,0:T(8,128)(2,1)S(1)}, u32[]{:S(2)}, u32[]{:S(2)}) collective-permute-start(bf16[208,1568]{1,0:T(8,128)(2,1)} %get-tuple-element.78.refs_0_), channel_id=1, source_target_pairs={{0,2},{1,3},{2,0},{3,1},{4,6},{5,7},{6,4},{7,5},{8,10},{9,11},{10,... | collective-permute-start | bytes 1956872 | tf_op jit(solution)/shard_map/ppermute | solution.py:624
  37.5 21.6 %copy-start.25 = (bf16[208,1568]{1,0:T(8,128)(2,1)}, bf16[208,1568]{1,0:T(8,128)(2,1)S(1)}, u32[]{:S(2)}) copy-start(bf16[208,1568]{1,0:T(8,128)(2,1)S(1)} %collective-permute-done.2.refs_0_) | copy-start | bytes 1956868
  37.5 21.6 %collective-permute-start.3 = (bf16[208,1568]{1,0:T(8,128)(2,1)S(1)}, bf16[208,1568]{1,0:T(8,128)(2,1)S(1)}, u32[]{:S(2)}, u32[]{:S(2)}) collective-permute-start(bf16[208,1568]{1,0:T(8,128)(2,1)S(1)} %collective-permute-done.2.refs_0_), channel_id=1, source_target_pairs={{0,1},{1,0},{2,3},{3,2},{4,5},{5,4},{6,7},{7,6},{8,9},{9,8},{10,11... | collective-permute-start | bytes 1956872 | tf_op jit(solution)/shard_map/ppermute | solution.py:624
  41.5 17.6 %copy-start.24 = (bf16[208,1568]{1,0:T(8,128)(2,1)}, bf16[208,1568]{1,0:T(8,128)(2,1)S(1)}, u32[]{:S(2)}) copy-start(bf16[208,1568]{1,0:T(8,128)(2,1)S(1)} %collective-permute-done.4.refs_0_) | copy-start | bytes 1956868
  41.5 35.1 %collective-permute-start.5 = (bf16[208,1568]{1,0:T(8,128)(2,1)S(1)}, bf16[208,1568]{1,0:T(8,128)(2,1)S(1)}, u32[]{:S(2)}, u32[]{:S(2)}) collective-permute-start(bf16[208,1568]{1,0:T(8,128)(2,1)S(1)} %collective-permute-done.4.refs_0_), channel_id=1, source_target_pairs={{0,1},{1,0},{2,3},{3,2},{4,5},{5,4},{6,7},{7,6},{8,9},{9,8},{10,11... | collective-permute-start | bytes 1956872 | tf_op jit(solution)/shard_map/ppermute | solution.py:624
  118.4 18.7 %collective-permute-start.8 = (bf16[2,960,384]{2,1,0:T(8,128)(2,1)}, bf16[2,960,384]{2,1,0:T(8,128)(2,1)S(1)}, u32[]{:S(2)}, u32[]{:S(2)}) collective-permute-start(bf16[2,960,384]{2,1,0:T(8,128)(2,1)} %get-tuple-element.105), channel_id=1, source_target_pairs={{0,1},{1,0},{2,3},{3,2},{4,5},{5,4},{6,7},{7,6},{8,9},{9,8},{10,11... | collective-permute-start | bytes 4423688 | tf_op jit(solution)/shard_map/ppermute | solution.py:624
  119.0 18.1 %copy-start.4 = (bf16[2,960,384]{2,1,0:T(8,128)(2,1)S(1)}, bf16[2,960,384]{2,1,0:T(8,128)(2,1)}, u32[]{:S(2)}) copy-start(bf16[2,960,384]{2,1,0:T(8,128)(2,1)} %get-tuple-element.104) | copy-start | bytes 4423684
  137.0 22.1 %collective-permute-start.6 = (bf16[192,1568]{1,0:T(8,128)(2,1)}, bf16[192,1568]{1,0:T(8,128)(2,1)S(1)}, u32[]{:S(2)}, u32[]{:S(2)}) collective-permute-start(bf16[192,1568]{1,0:T(8,128)(2,1)} %get-tuple-element.93), channel_id=1, source_target_pairs={{0,1},{1,0},{2,3},{3,2},{4,5},{5,4},{6,7},{7,6},{8,9},{9,8},{10,11... | collective-permute-start | bytes 1806344 | tf_op jit(solution)/shard_map/ppermute | solution.py:624
  138.6 18.6 %copy-start.1 = (bf16[2,960,384]{2,1,0:T(8,128)(2,1)S(1)}, bf16[2,960,384]{2,1,0:T(8,128)(2,1)}, u32[]{:S(2)}) copy-start(bf16[2,960,384]{2,1,0:T(8,128)(2,1)} %add_convert_fusion.refs_10_) | copy-start | bytes 4423684
  156.7 3.1 %collective-permute-start.11 = (bf16[192,1568]{1,0:T(8,128)(2,1)}, bf16[192,1568]{1,0:T(8,128)(2,1)S(1)}, u32[]{:S(2)}, u32[]{:S(2)}) collective-permute-start(bf16[192,1568]{1,0:T(8,128)(2,1)} %get-tuple-element.110), channel_id=1, source_target_pairs={{0,1},{1,0},{2,3},{3,2},{4,5},{5,4},{6,7},{7,6},{8,9},{9,8},{10,11... | collective-permute-start | bytes 1806344 | tf_op jit(solution)/shard_map/ppermute | solution.py:624
  157.3 19.4 %collective-permute-start.9 = (bf16[960,384]{1,0:T(8,128)(2,1)S(1)}, bf16[960,384]{1,0:T(8,128)(2,1)S(1)}, u32[]{:S(2)}, u32[]{:S(2)}) collective-permute-start(bf16[960,384]{1,0:T(8,128)(2,1)S(1)} %slice_bitcast_fusion), channel_id=1, source_target_pairs={{0,2},{1,3},{2,0},{3,1},{4,6},{5,7},{6,4},{7,5},{8,10},{9,11},{10,... | collective-permute-start | bytes 2211848 | tf_op jit(solution)/shard_map/ppermute | solution.py:624
  159.3 17.6 %copy-start.7 = (bf16[192,1568]{1,0:T(8,128)(2,1)}, bf16[192,1568]{1,0:T(8,128)(2,1)S(1)}, u32[]{:S(2)}) copy-start(bf16[192,1568]{1,0:T(8,128)(2,1)S(1)} %add_convert_fusion.2.refs_11_) | copy-start | bytes 1806340
  159.3 40.7 %collective-permute-start.7 = (bf16[192,1568]{1,0:T(8,128)(2,1)S(1)}, bf16[192,1568]{1,0:T(8,128)(2,1)S(1)}, u32[]{:S(2)}, u32[]{:S(2)}) collective-permute-start(bf16[192,1568]{1,0:T(8,128)(2,1)S(1)} %add_convert_fusion.2.refs_11_), channel_id=1, source_target_pairs={{0,2},{1,3},{2,0},{3,1},{4,6},{5,7},{6,4},{7,5},{8,10},{9,11},{10,... | collective-permute-start | bytes 1806344 | tf_op jit(solution)/shard_map/ppermute | solution.py:624
  160.0 60.5 %collective-permute-start.12 = (bf16[192,1568]{1,0:T(8,128)(2,1)S(1)}, bf16[192,1568]{1,0:T(8,128)(2,1)}, u32[]{:S(2)}, u32[]{:S(2)}) collective-permute-start(bf16[192,1568]{1,0:T(8,128)(2,1)S(1)} %add_convert_fusion.1.refs_12_), channel_id=1, source_target_pairs={{0,2},{1,3},{2,0},{3,1},{4,6},{5,7},{6,4},{7,5},{8,10},{9,11},{10,... | collective-permute-start | bytes 1806344 | tf_op jit(solution)/shard_map/ppermute | solution.py:624
  177.0 20.0 %collective-permute-start.13 = (bf16[480,384]{1,0:T(8,128)(2,1)S(1)}, bf16[480,384]{1,0:T(8,128)(2,1)S(1)}, u32[]{:S(2)}, u32[]{:S(2)}) collective-permute-start(bf16[480,384]{1,0:T(8,128)(2,1)S(1)} %broadcast_select_fusion), channel_id=1, source_target_pairs={{0,4},{4,0},{8,12},{12,8},{16,20},{20,16},{24,28},{28,24},{1,5},{5... | collective-permute-start | bytes 1105928 | tf_op jit(solution)/shard_map/ppermute | solution.py:629
  198.3 20.4 %collective-permute-start.15 = (bf16[240,384]{1,0:T(8,128)(2,1)S(1)}, bf16[240,384]{1,0:T(8,128)(2,1)S(1)}, u32[]{:S(2)}, u32[]{:S(2)}) collective-permute-start(bf16[240,384]{1,0:T(8,128)(2,1)S(1)} %broadcast_select_fusion.1), channel_id=1, source_target_pairs={{0,8},{4,12},{8,0},{12,4},{16,24},{20,28},{24,16},{28,20},{1,9},{5... | collective-permute-start | bytes 552968 | tf_op jit(solution)/shard_map/ppermute | solution.py:629
  226.3 1.7 collective-permute-start.16
  229.1 5.4 %collective-permute-start.17 = (bf16[160,384]{1,0:T(8,128)(2,1)S(1)}, bf16[160,384]{1,0:T(8,128)(2,1)S(1)}, u32[]{:S(2)}, u32[]{:S(2)}) collective-permute-start(bf16[160,384]{1,0:T(8,128)(2,1)S(1)} %slice_bitcast_fusion.4), channel_id=1, source_target_pairs={{0,2},{1,3},{2,0},{3,1},{4,6},{5,7},{6,4},{7,5},{8,10},{9,11},{10,... | collective-permute-start | bytes 368648 | tf_op jit(solution)/shard_map/ppermute | solution.py:624
  232.5 22.9 %collective-permute-start.10 = (bf16[192,1568]{1,0:T(8,128)(2,1)S(1)}, bf16[192,1568]{1,0:T(8,128)(2,1)S(1)}, u32[]{:S(2)}, u32[]{:S(2)}) collective-permute-start(bf16[192,1568]{1,0:T(8,128)(2,1)S(1)} %copy-done.29), channel_id=1, source_target_pairs={{0,1},{1,0},{2,3},{3,2},{4,5},{5,4},{6,7},{7,6},{8,9},{9,8},{10,11... | collective-permute-start | bytes 1806344 | tf_op jit(solution)/shard_map/ppermute | solution.py:624
  232.6 22.9 %collective-permute-start.14 = (bf16[192,1568]{1,0:T(8,128)(2,1)S(1)}, bf16[192,1568]{1,0:T(8,128)(2,1)S(1)}, u32[]{:S(2)}, u32[]{:S(2)}) collective-permute-start(bf16[192,1568]{1,0:T(8,128)(2,1)S(1)} %copy-done.30), channel_id=1, source_target_pairs={{0,1},{1,0},{2,3},{3,2},{4,5},{5,4},{6,7},{7,6},{8,9},{9,8},{10,11... | collective-permute-start | bytes 1806344 | tf_op jit(solution)/shard_map/ppermute | solution.py:624
  234.5 4.3 %collective-permute-start.18 = (bf16[80,384]{1,0:T(8,128)(2,1)S(1)}, bf16[80,384]{1,0:T(8,128)(2,1)S(1)}, u32[]{:S(2)}, u32[]{:S(2)}) collective-permute-start(bf16[80,384]{1,0:T(8,128)(2,1)S(1)} %broadcast_select_fusion.3), channel_id=1, source_target_pairs={{0,4},{4,0},{8,12},{12,8},{16,20},{20,16},{24,28},{28,24},{1,5},{5... | collective-permute-start | bytes 184328 | tf_op jit(solution)/shard_map/ppermute | solution.py:629
  235.4 6.4 %collective-permute-start.23 = (bf16[120,384]{1,0:T(8,128)(2,1)S(1)}, bf16[120,384]{1,0:T(8,128)(2,1)S(1)}, u32[]{:S(2)}, u32[]{:S(2)}) collective-permute-start(bf16[120,384]{1,0:T(8,128)(2,1)S(1)} %broadcast_select_fusion.2), channel_id=1, source_target_pairs={{0,16},{4,20},{8,24},{12,28},{16,0},{20,4},{24,8},{28,12},{1,17},{... | collective-permute-start | bytes 276488 | tf_op jit(solution)/shard_map/ppermute | solution.py:629
  238.9 4.8 %collective-permute-start.19 = (bf16[40,384]{1,0:T(8,128)(2,1)S(1)}, bf16[40,384]{1,0:T(8,128)(2,1)S(1)}, u32[]{:S(2)}, u32[]{:S(2)}) collective-permute-start(bf16[40,384]{1,0:T(8,128)(2,1)S(1)} %broadcast_select_fusion.4), channel_id=1, source_target_pairs={{0,8},{4,12},{8,0},{12,4},{16,24},{20,28},{24,16},{28,20},{1,9},{5... | collective-permute-start | bytes 92168 | tf_op jit(solution)/shard_map/ppermute | solution.py:629
  241.8 5.6 %collective-permute-start.24 = (bf16[120,384]{1,0:T(8,128)(2,1)S(1)}, bf16[120,384]{1,0:T(8,128)(2,1)S(1)}, u32[]{:S(2)}, u32[]{:S(2)}) collective-permute-start(bf16[120,384]{1,0:T(8,128)(2,1)S(1)} %add_convert_fusion.6), channel_id=1, source_target_pairs={{0,16},{4,20},{8,24},{12,28},{16,0},{20,4},{24,8},{28,12},{1,17},{... | collective-permute-start | bytes 276488 | tf_op jit(solution)/shard_map/ppermute | solution.py:629
  243.7 5.2 %collective-permute-start.20 = (bf16[40,384]{1,0:T(8,128)(2,1)S(1)}, bf16[40,384]{1,0:T(8,128)(2,1)S(1)}, u32[]{:S(2)}, u32[]{:S(2)}) collective-permute-start(bf16[40,384]{1,0:T(8,128)(2,1)S(1)} %add_convert_fusion.9), channel_id=1, source_target_pairs={{0,16},{4,20},{8,24},{12,28},{16,0},{20,4},{24,8},{28,12},{1,17},{... | collective-permute-start | bytes 92168 | tf_op jit(solution)/shard_map/ppermute | solution.py:629
  247.5 5.6 %collective-permute-start.25 = (bf16[240,384]{1,0:T(8,128)(2,1)S(1)}, bf16[240,384]{1,0:T(8,128)(2,1)S(1)}, u32[]{:S(2)}, u32[]{:S(2)}) collective-permute-start(bf16[240,384]{1,0:T(8,128)(2,1)S(1)} %maximum_select_fusion.2), channel_id=1, source_target_pairs={{0,8},{4,12},{8,0},{12,4},{16,24},{20,28},{24,16},{28,20},{1,9},{5... | collective-permute-start | bytes 552968 | tf_op jit(solution)/shard_map/ppermute | solution.py:629
  248.9 5.8 %collective-permute-start.21 = (bf16[40,384]{1,0:T(8,128)(2,1)S(1)}, bf16[40,384]{1,0:T(8,128)(2,1)S(1)}, u32[]{:S(2)}, u32[]{:S(2)}) collective-permute-start(bf16[40,384]{1,0:T(8,128)(2,1)S(1)} %add_convert_fusion.8), channel_id=1, source_target_pairs={{0,8},{4,12},{8,0},{12,4},{16,24},{20,28},{24,16},{28,20},{1,9},{5... | collective-permute-start | bytes 92168 | tf_op jit(solution)/shard_map/ppermute | solution.py:629
  253.3 20.5 %collective-permute-start.26 = (bf16[480,384]{1,0:T(8,128)(2,1)S(1)}, bf16[480,384]{1,0:T(8,128)(2,1)S(1)}, u32[]{:S(2)}, u32[]{:S(2)}) collective-permute-start(bf16[480,384]{1,0:T(8,128)(2,1)S(1)} %maximum_select_fusion.1), channel_id=1, source_target_pairs={{0,4},{4,0},{8,12},{12,8},{16,20},{20,16},{24,28},{28,24},{1,5},{5... | collective-permute-start | bytes 1105928 | tf_op jit(solution)/shard_map/ppermute | solution.py:629
  254.6 17.0 %collective-permute-start.22 = (bf16[80,384]{1,0:T(8,128)(2,1)S(1)}, bf16[80,384]{1,0:T(8,128)(2,1)S(1)}, u32[]{:S(2)}, u32[]{:S(2)}) collective-permute-start(bf16[80,384]{1,0:T(8,128)(2,1)S(1)} %maximum_select_fusion.4), channel_id=1, source_target_pairs={{0,4},{4,0},{8,12},{12,8},{16,20},{20,16},{24,28},{28,24},{1,5},{5... | collective-permute-start | bytes 184328 | tf_op jit(solution)/shard_map/ppermute | solution.py:629
  (28 other events, 128.8 us)

commit v2 on v1

v2 whole, which is shorter than its diff:
```python
import functools

import jax
import jax.numpy as jnp
from jax import lax
from jax.experimental import pallas as pl
from jax.experimental.pallas import tpu as pltpu
from jax.sharding import PartitionSpec as P

D_IN = 192
D_OUT = 384
HEADS = 4
HEAD_DIM = 96
FF = 1536
LANES = 128
EXT = 208
SCALE = HEAD_DIM**-0.5
LOG2E = 1.4426950408889634
BF = jnp.bfloat16
F32 = jnp.float32
VMEM_BYTES = 64 * 2**20
FF_BLOCK = 768


def mm(a, b, ca, cb):
    return lax.dot_general(a, b, (((ca,), (cb,)), ((), ())), preferred_element_type=F32)


def iota(shape, dim):
    return lax.broadcasted_iota(jnp.int32, shape, dim)


def call(body, grid, ins, outs, scratch=(), name=None, cost=None, after=(), aliases=None):
    count = len(ins)

    def run(*refs):
        body(*refs[:count], *refs[count + len(after) :])

    ins = [*ins, *((pl.BlockSpec(memory_space=pl.ANY), value) for value in after)]
    return pl.pallas_call(
        run,
        grid=grid,
        in_specs=[spec for spec, _ in ins],
        out_specs=[spec for spec, _, _ in outs],
        out_shape=[jax.ShapeDtypeStruct(shape, dtype) for _, shape, dtype in outs],
        scratch_shapes=list(scratch),
        compiler_params=pltpu.CompilerParams(
            dimension_semantics=("arbitrary",) * len(grid), vmem_limit_bytes=VMEM_BYTES
        ),
        name=name,
        cost_estimate=pl.CostEstimate(
            flops=int(cost * 1.1e9), bytes_accessed=int(cost * 1e6), transcendentals=0
        ),
        input_output_aliases=aliases or {},
    )(*[value for _, value in ins])


def whole(value):
    rank = len(value.shape)
    return (pl.BlockSpec(value.shape, lambda *_: (0,) * rank), value)


def part(value):
    rank = len(value.shape)
    return (pl.BlockSpec((1,) + value.shape[1:], lambda i: (i,) + (0,) * (rank - 1)), value)


def at_clip(value, clip):
    rank = len(value.shape)
    return (pl.BlockSpec((1,) + value.shape[1:], lambda *_: (clip,) + (0,) * (rank - 1)), value)


def at_head(value, clip):
    rank = len(value.shape)
    return (
        pl.BlockSpec((None, 1) + value.shape[2:], lambda i: (clip, i) + (0,) * (rank - 2)),
        value,
    )


def out_part(shape, dtype):
    rank = len(shape)
    return (pl.BlockSpec((1,) + shape[1:], lambda i: (i,) + (0,) * (rank - 1)), shape, dtype)


def out_whole(shape, dtype):
    rank = len(shape)
    return (pl.BlockSpec(shape, lambda *_: (0,) * rank), shape, dtype)


def line(ref):
    return ref[...].astype(F32).reshape(1, -1)


def eye(size):
    return jnp.where(iota((size, size), 0) == iota((size, size), 1), 1.0, 0.0).astype(BF)


def column(ref):
    size = ref.shape[0]
    values = jnp.broadcast_to(line(ref), (16, size)).astype(BF)
    return mm(eye(size), values, 1, 1)[:, 0:1]


def normed_body(clip, tok_ref, frames_ref, counts_ref, gain_ref, shift_ref, nt_ref, pooled_ref):
    slots, _, units = tok_ref.shape[1:]
    gain, shift = column(gain_ref), column(shift_ref)
    x = jnp.concatenate([tok_ref[0, s].astype(F32) for s in range(slots)], axis=1)
    center = x - jnp.mean(x, axis=0, keepdims=True)
    var = jnp.mean(center * center, axis=0, keepdims=True)
    normed = (center * lax.rsqrt(var + 1e-06) * gain + shift).astype(BF)
    nt_ref[:D_IN, :] = normed
    normed = normed.astype(F32)
    pieces = [normed[:, units * s : units * (s + 1)] for s in range(slots)]
    extra = iota((EXT - D_IN, units), 0)
    invalid = jnp.where(frames_ref[clip : clip + 1, :] >= counts_ref[clip], 1.0, 0.0)
    extra = jnp.where(extra == 0, 1.0, jnp.where(extra == 1, invalid, 0.0))
    nt_ref[D_IN:, :] = jnp.concatenate([extra] * slots, axis=1).astype(BF)
    means = []
    for p in range(4):
        first = 8 * (p >> 1) + 2 * (p & 1)
        means.append(
            (pieces[first] + pieces[first + 1] + pieces[first + 4] + pieces[first + 5]) * 0.25
        )
    pooled = jnp.concatenate(means, axis=1)
    row = iota((2 * LANES - D_IN, 4 * units), 0)
    pooled = jnp.concatenate([pooled, jnp.where(row == 0, 1.0, 0.0)], axis=0)
    pooled_ref[...] = pooled.T.astype(BF)


def normed_tokens(clip, tokens, frames, counts, gain, shift):
    _, slots, _, units = tokens.shape
    return call(
        functools.partial(normed_body, clip),
        (1,),
        [
            at_clip(tokens, clip),
            whole(frames),
            (pl.BlockSpec(memory_space=pltpu.SMEM), counts),
            whole(gain),
            whole(shift),
        ],
        [out_whole((EXT, slots * units), BF), out_whole((4 * units, 2 * LANES), BF)],
        name="normed",
        cost=3,
    )


def query_body(clips, qkv_ref, wp_ref, qbias_ref, vbias_ref, *refs):
    pooled_refs, wt_ref, wg_ref, q_refs = refs[:clips], refs[clips], refs[clips + 1], refs[clips + 2 :]
    bias = jnp.concatenate(
        [line(qbias_ref), jnp.zeros((1, D_OUT), F32), line(vbias_ref)], axis=1
    )
    bias = jnp.where(iota((EXT - D_IN, 3 * D_OUT), 0) == 0, bias, 0.0).astype(BF)
    extended = jnp.concatenate([qkv_ref[...], bias], axis=0)
    tall = jnp.where(iota((LANES, HEAD_DIM), 0) == iota((LANES, HEAD_DIM), 1), 1.0, 0.0).astype(BF)
    row, lane = iota((LANES, EXT), 0), iota((LANES, EXT), 1)
    ones = (lane == D_IN) & (row >= HEAD_DIM)
    extras = (
        jnp.where(ones & (row == HEAD_DIM), 8.0, 0.0),
        jnp.where(
            (lane == D_IN + 1) & (row == HEAD_DIM),
            -1e30,
            jnp.where(ones & (row == HEAD_DIM + 1), 1.0, 0.0),
        ),
        jnp.where(ones & (row <= HEAD_DIM + 1), 1.0, 0.0),
    )
    for block in range(3 * HEADS):
        columns = extended[:, HEAD_DIM * block : HEAD_DIM * (block + 1)]
        wt_ref[block, :, :EXT] = (mm(tall, columns, 1, 1) + extras[block // HEADS]).astype(BF)
        wt_ref[block, :, EXT:] = jnp.zeros((LANES, 2 * LANES - EXT), BF)
    wg_ref[...] = jnp.concatenate(
        [
            qkv_ref[:, start : start + HEAD_DIM]
            for h in range(HEADS)
            for start in (D_OUT + HEAD_DIM * h, 2 * D_OUT + HEAD_DIM * h)
        ],
        axis=1,
    )
    for block in range(D_OUT // LANES):
        columns = wp_ref[:, LANES * block : LANES * (block + 1)]
        wt_ref[3 * HEADS + block, :, :D_IN] = mm(eye(LANES), columns, 1, 1).astype(BF)
        wt_ref[3 * HEADS + block, :, D_IN:] = jnp.zeros((LANES, 2 * LANES - D_IN), BF)
    for c in range(clips):
        pooled = pooled_refs[c][...]
        for h in range(HEADS):
            q_refs[2 * c][h] = (mm(pooled, wt_ref[h], 1, 1) * (SCALE * LOG2E)).astype(BF)
            q_refs[2 * c + 1][h] = (mm(wt_ref[h, :HEAD_DIM], pooled, 1, 1) * SCALE).astype(BF)


def queries_of(qkv, wp, qbias, vbias, pooled):
    clips, count = len(pooled), pooled[0].shape[0]
    wt, wg, *rest = call(
        functools.partial(query_body, clips),
        (1,),
        [whole(v) for v in (qkv, wp, qbias, vbias, *pooled)],
        [
            out_whole((3 * HEADS + D_OUT // LANES, LANES, 2 * LANES), BF),
            out_whole((D_IN, 2 * D_OUT), BF),
            *[
                out_whole((HEADS, count, LANES), BF),
                out_whole((HEADS, HEAD_DIM, count), BF),
            ]
            * clips,
        ],
        name="queries",
        cost=5,
    )
    return wt, wg, [(rest[2 * c], rest[2 * c + 1]) for c in range(clips)]


def forward_body(na_ref, nb_ref, wt_ref, qs_ref, p_ref, kt_ref, vt_ref, o_ref, n_ref):
    rows = na_ref.shape[1]
    queries = qs_ref.shape[1]

    @pl.when(pl.program_id(0) == 0)
    def _():
        n_ref[:, :rows] = na_ref[...]
        n_ref[:, rows:] = nb_ref[...]

    h = pl.program_id(0)
    lane = iota((queries, LANES), 1)
    bound_lane = lane == HEAD_DIM + 1
    pick = (iota((16, LANES), 0) == 0) & (iota((16, LANES), 1) == HEAD_DIM + 1)
    pick = jnp.where(pick, 1.0, 0.0).astype(BF)
    tall = HEAD_DIM + 16
    kt = mm(wt_ref[HEADS + h][:, :EXT], n_ref[...], 1, 0)
    vt = mm(wt_ref[2 * HEADS + h][:, :EXT], n_ref[...], 1, 0).astype(BF)
    plain = kt[:HEAD_DIM]
    longest = jnp.max(jnp.sum(plain * plain, axis=0, keepdims=True), axis=1, keepdims=True)
    kt = kt.astype(BF)
    kt_ref[0] = kt
    vt_ref[0] = vt
    q = qs_ref[0].astype(F32)
    norm = jnp.sum(jnp.where(lane < HEAD_DIM, q * q, 0.0), axis=1, keepdims=True)
    q = jnp.where(bound_lane, -jnp.sqrt(norm * longest), q).astype(BF)
    p = jnp.exp2(mm(q, kt, 1, 0)).astype(BF)
    p_ref[0] = p
    o = mm(vt[:tall], p, 1, 1)
    o_ref[0, :tall] = o
    o_ref[0, tall:] = mm(pick, q, 1, 1)

    @pl.when(jnp.min(o[HEAD_DIM : HEAD_DIM + 1]) < 1e-27)
    def _():
        s = mm(qs_ref[0], kt_ref[0], 1, 0)
        m = jnp.max(s, axis=1, keepdims=True).astype(BF).astype(F32)
        again = jnp.exp2(s - m).astype(BF)
        p_ref[0] = again
        o_ref[0, :tall] = mm(vt_ref[0, :tall], again, 1, 1)
        o_ref[0, tall:] = mm(
            pick, jnp.where(bound_lane, -m, qs_ref[0].astype(F32)).astype(BF), 1, 1
        )


def forward(na, nb, wt, qs, after=()):
    rows = na.shape[1]
    queries = qs.shape[1]
    return call(
        forward_body,
        (HEADS,),
        [whole(na), whole(nb), whole(wt), part(qs)],
        [
            out_part((HEADS, queries, 2 * rows), BF),
            out_part((HEADS, LANES, 2 * rows), BF),
            out_part((HEADS, LANES, 2 * rows), BF),
            out_part((HEADS, LANES, queries), F32),
        ],
        [pltpu.VMEM((EXT, 2 * rows), BF)],
        name="attend",
        after=after,
        cost=12,
    )


def middle_body(clips, me_ref, *refs):
    o1_refs, o2_refs, pooled_refs = refs[:clips], refs[clips : 2 * clips], refs[2 * clips : 3 * clips]
    up_ref, bproj_ref, bout_ref, gain_ref, shift_ref, bshrink_ref, bexpand_ref = refs[
        3 * clips : 3 * clips + 7
    ]
    wp_ref, wo_ref, we_ref, ws_ref = refs[3 * clips + 7 : 3 * clips + 11]
    out_ref, hg_ref, attended_ref, factor_ref = refs[3 * clips + 11 : 3 * clips + 15]
    shard_refs, wpt_ref = refs[3 * clips + 15 : 3 * clips + 19], refs[3 * clips + 19]
    we_acc, ws_acc, wo_acc, wp_acc, misc_acc = refs[3 * clips + 20 :]
    queries = pooled_refs[0].shape[0]
    rows = [slice(queries * c, queries * (c + 1)) for c in range(clips)]
    heads = [[] for _ in range(clips)]
    for c in range(clips):
        for h in range(HEADS):
            o1, o2 = o1_refs[c][h], o2_refs[c][h]
            l1, l2 = o1[HEAD_DIM : HEAD_DIM + 1], o2[HEAD_DIM : HEAD_DIM + 1]
            m1, m2 = -o1[HEAD_DIM + 16 : HEAD_DIM + 17], -o2[HEAD_DIM + 16 : HEAD_DIM + 17]
            m = jnp.maximum(m1, m2)
            a1, a2 = jnp.exp2(m1 - m), jnp.exp2(m2 - m)
            inverse = 1.0 / (a1 * l1 + a2 * l2)
            c1, c2 = a1 * inverse, a2 * inverse
            heads[c].append(o1[:HEAD_DIM] * c1 + o2[:HEAD_DIM] * c2)
            attended_ref[c, h] = heads[c][h]
            factor_ref[c, h] = jnp.concatenate([c1, c2, jnp.zeros((6, queries), F32)], axis=0)
    attended = jnp.concatenate([jnp.concatenate(parts, axis=0).T for parts in heads], axis=0)
    attended = attended.astype(BF)
    pooled = jnp.concatenate([ref[...].astype(F32) for ref in pooled_refs], axis=0).astype(BF)
    up = jnp.concatenate([up_ref[c].astype(F32) for c in range(clips)], axis=0)
    up_low = up.astype(BF)
    hidden = mm(pooled[:, :D_IN], wp_ref[...], 1, 0) + line(bproj_ref)
    hidden = hidden + mm(attended, wo_ref[...], 1, 0) + line(bout_ref)
    center = hidden - jnp.mean(hidden, axis=1, keepdims=True)
    inv_std = lax.rsqrt(jnp.mean(center * center, axis=1, keepdims=True) + 1e-06)
    n = center * inv_std
    gain2 = line(gain_ref)
    second = (n * gain2 + line(shift_ref)).astype(BF)
    out = hidden + line(bshrink_ref)
    second_grad = jnp.zeros(out.shape, F32)
    bexpand = line(bexpand_ref)
    for start in range(0, FF, FF_BLOCK):
        block = slice(start, start + FF_BLOCK)
        before = mm(second, we_ref[:, block], 1, 0) + bexpand[:, block]
        cdf = 0.5 + 0.5 * lax.erf(before * (0.5**0.5))
        active = (before * cdf).astype(BF)
        out = out + mm(active, ws_ref[block, :], 1, 0)
        slope = cdf + before * (jnp.exp(before * before * -0.5) * (0.5 / jnp.pi) ** 0.5)
        before_grad = (mm(up_low, ws_ref[block, :], 1, 1) * slope).astype(BF)
        ws_acc[:, block] = mm(up_low, active, 0, 0)
        we_acc[:, block] = mm(second, before_grad, 0, 0)
        second_grad = second_grad + mm(before_grad, we_ref[:, block], 1, 1)
        misc_acc[0:1, block] = jnp.sum(before_grad.astype(F32), axis=0, keepdims=True)
    for c in range(clips):
        out_ref[c] = out[rows[c]]
    e = gain2 * second_grad
    back = (
        e - jnp.mean(e, axis=1, keepdims=True) - n * jnp.mean(e * n, axis=1, keepdims=True)
    ) * inv_std
    hidden_full = (up + back).astype(BF).astype(F32)
    hidden_grad = hidden_full.astype(BF)
    wo_acc[...] = mm(hidden_grad, attended, 0, 0)
    wp_acc[...] = mm(hidden_grad, pooled, 0, 0)
    misc_acc[1:2, :D_OUT] = jnp.sum(second_grad * n, axis=0, keepdims=True)
    misc_acc[2:3, :D_OUT] = jnp.sum(second_grad, axis=0, keepdims=True)
    misc_acc[3:4, :D_OUT] = jnp.sum(up, axis=0, keepdims=True)
    misc_acc[4:5, :D_OUT] = jnp.sum(hidden_full, axis=0, keepdims=True)
    for c in range(clips):
        hg_ref[c] = hidden_full[rows[c]].astype(BF)
    me = me_ref[0]
    wpt_ref[...] = wp_acc[...]
    for u in range(4):
        for k in range(4):
            misc_acc[8 + u : 9 + u, HEAD_DIM * k : HEAD_DIM * (k + 1)] = misc_acc[
                1 + k : 2 + k, HEAD_DIM * u : HEAD_DIM * (u + 1)
            ]
    for r in range(4):
        u = me ^ r
        ref = shard_refs[r]
        wide = pl.ds(pl.multiple_of(u * 384, LANES), 384)
        tall = pl.ds(pl.multiple_of(u * 96, 8), 96)
        ref[0:384, :] = we_acc[:, wide].astype(BF)
        ref[384:768, :] = ws_acc[:, wide].astype(BF)
        ref[768:864, :] = wo_acc[tall, :].astype(BF)
        wp = wp_acc[tall, :]
        ref[864:912, :] = jnp.concatenate([wp[:48, :D_IN], wp[48:, :D_IN]], axis=1).astype(BF)
        bias = misc_acc[0:1, wide]
        others = misc_acc[pl.ds(8 + u, 1), :384]
        row = iota((48, 384), 0)
        ref[912:960, :] = jnp.where(row == 0, bias, jnp.where(row == 1, others, 0.0)).astype(BF)


def middle(me, o1, o2, pooled, up, vectors, weights):
    clips = len(pooled)
    queries = pooled[0].shape[0]
    return call(
        functools.partial(middle_body, clips),
        (1,),
        [
            (pl.BlockSpec(memory_space=pltpu.SMEM), me),
            *(whole(value) for value in (*o1, *o2, *pooled, up, *vectors, *weights)),
        ],
        [
            out_whole((clips, queries, D_OUT), F32),
            out_whole((clips, queries, D_OUT), BF),
            out_whole((clips, HEADS, HEAD_DIM, queries), F32),
            out_whole((clips, HEADS, 8, queries), F32),
            *([out_whole((960, 384), BF)] * 4),
            out_whole((D_OUT, 2 * LANES), F32),
        ],
        [
            pltpu.VMEM((D_OUT, FF), F32),
            pltpu.VMEM((D_OUT, FF), F32),
            pltpu.VMEM((D_OUT, D_OUT), F32),
            pltpu.VMEM((D_OUT, 2 * LANES), F32),
            pltpu.VMEM((16, FF), F32),
        ],
        name="middle",
        cost=16,
    )


def attended_grad_body(hg_ref, attended_ref, factor_ref, wo_ref, do1_ref, do2_ref, do1t_ref, do2t_ref):
    queries = hg_ref.shape[1]
    row = iota((LANES - HEAD_DIM, queries), 0)
    grad = mm(wo_ref[...], hg_ref[0], 1, 1).astype(BF).astype(F32)
    for h in range(HEADS):
        own = grad[HEAD_DIM * h : HEAD_DIM * (h + 1)]
        for k, do_ref, dot_ref in ((0, do1_ref, do1t_ref), (1, do2_ref, do2t_ref)):
            scaled = (own * factor_ref[0, h, k : k + 1]).astype(BF)
            dot_ref[0, h] = scaled
            scaled = scaled.astype(F32)
            inner = jnp.sum(scaled * attended_ref[0, h], axis=0, keepdims=True)
            high = inner.astype(BF).astype(F32)
            extra = jnp.where(row == 0, -high, jnp.where(row == 1, high - inner, 0.0))
            do_ref[0, h] = jnp.concatenate([scaled, extra], axis=0).T.astype(BF)


def attended_grads(hg, attended, factors, wo):
    clips, queries, _ = hg.shape
    grad = (clips, HEADS, queries, LANES)
    grad_t = (clips, HEADS, HEAD_DIM, queries)
    return call(
        attended_grad_body,
        (clips,),
        [part(hg), part(attended), part(factors), whole(wo)],
        [out_part(grad, BF), out_part(grad, BF), out_part(grad_t, BF), out_part(grad_t, BF)],
        name="attended_grads",
        cost=5,
    )


def backward_body(
    na_ref,
    nb_ref,
    wg_ref,
    p_ref,
    kt_ref,
    vt_ref,
    do_ref,
    dot_ref,
    qt_ref,
    dq_ref,
    dw_ref,
    ga_ref,
    gb_ref,
    n_ref,
    both_ref,
):
    rows = na_ref.shape[1]
    h = pl.program_id(0)
    p = p_ref[0]
    ds = p * mm(do_ref[0], vt_ref[0], 1, 0).astype(BF)
    dq_ref[0] = mm(kt_ref[0, :HEAD_DIM], ds, 1, 1)
    both_ref[h, :HEAD_DIM] = mm(qt_ref[0], ds, 1, 0).astype(BF)
    both_ref[h, HEAD_DIM:] = mm(dot_ref[0], p, 1, 0).astype(BF)

    @pl.when(h == HEADS - 1)
    def _():
        n_ref[:, :rows] = na_ref[...]
        n_ref[:, rows:] = nb_ref[...]
        both = both_ref[...].reshape(2 * D_OUT, 2 * rows)
        dw_ref[...] = mm(both, n_ref[...], 1, 1)
        g = mm(wg_ref[...], both, 1, 0).astype(BF)
        ga_ref[...] = g[:, :rows]
        gb_ref[...] = g[:, rows:]


def backward(clip, na, nb, wg, p, kt, vt, do, dot, qt, after=()):
    rows = na.shape[1]
    queries = qt.shape[2]
    return call(
        backward_body,
        (HEADS,),
        [
            whole(na),
            whole(nb),
            whole(wg),
            part(p),
            part(kt),
            part(vt),
            at_head(do, clip),
            at_head(dot, clip),
            part(qt),
        ],
        [
            out_part((HEADS, HEAD_DIM, queries), F32),
            out_whole((2 * D_OUT, EXT), F32),
            out_whole((D_IN, rows), BF),
            out_whole((D_IN, rows), BF),
        ],
        [pltpu.VMEM((EXT, 2 * rows), BF), pltpu.VMEM((HEADS, 2 * HEAD_DIM, 2 * rows), BF)],
        name="attend_back",
        after=after,
        cost=17,
    )


def gather_body(clips, me_ref, *refs):
    dq_refs, dw_refs, pooled_refs = (
        refs[: 2 * clips],
        refs[2 * clips : 4 * clips],
        refs[4 * clips : 5 * clips],
    )
    wt_ref, wpt_ref, gain_ref, shift_ref = refs[5 * clips : 5 * clips + 4]
    shard_refs, (dw_acc, line_ref, shard_ref) = refs[5 * clips + 4 : 5 * clips + 8], refs[5 * clips + 8 :]
    total = dw_refs[0][...]
    for ref in dw_refs[1:]:
        total = total + ref[...]
    for h in range(HEADS):
        at = 2 * HEAD_DIM * h
        dw_acc[HEADS + h] = total[at : at + HEAD_DIM]
        dw_acc[2 * HEADS + h] = total[at + HEAD_DIM : at + 2 * HEAD_DIM]
    dw = None
    for c in range(clips):
        dq = (dq_refs[2 * c][...] + dq_refs[2 * c + 1][...]) * SCALE
        dq = dq.reshape(D_OUT, dq.shape[2]).astype(BF)
        term = mm(dq, pooled_refs[c][...], 1, 0)
        dw = term if dw is None else dw + term
    for h in range(HEADS):
        dw_acc[h] = dw[HEAD_DIM * h : HEAD_DIM * (h + 1), :EXT]
    gain_sum = jnp.zeros((1, D_IN), F32)
    shift_sum = jnp.zeros((1, D_IN), F32)
    wp = wt_ref[3 * HEADS :].reshape(D_OUT, 2 * LANES)[:, :D_IN]
    terms = [(wt_ref[b][:HEAD_DIM, :D_IN], dw_acc[b]) for b in range(3 * HEADS)]
    for w, dw in [*terms, (wp, wpt_ref[...])]:
        w = w.astype(F32)
        gain_sum = gain_sum + jnp.sum(w * dw[:, :D_IN], axis=0, keepdims=True)
        shift_sum = shift_sum + jnp.sum(w * dw[:, D_IN : D_IN + 1], axis=0, keepdims=True)
    gain_sum = (gain_sum - line(shift_ref) * shift_sum) / line(gain_ref)
    for at, first in ((0, 0), (1, 2 * HEADS)):
        for h in range(HEADS):
            sums = dw_acc[first + h][:, LANES:]
            sums = jnp.concatenate(
                [sums, jnp.zeros((HEAD_DIM, 2 * LANES - EXT), F32)], axis=1
            )
            sums = jnp.concatenate([sums, jnp.zeros((LANES - HEAD_DIM, LANES), F32)], axis=0).T
            line_ref[at : at + 1, HEAD_DIM * h : HEAD_DIM * (h + 1)] = sums[
                D_IN - LANES : D_IN - LANES + 1, :HEAD_DIM
            ]
    line_ref[2:3, :D_IN] = gain_sum
    line_ref[3:4, :D_IN] = shift_sum
    for u in range(4):
        at = 0
        for source, size in ((0, 96), (1, 96), (2, 48), (3, 48)):
            shard_ref[u : u + 1, at : at + size] = line_ref[
                source : source + 1, size * u : size * (u + 1)
            ]
            at += size
        shard_ref[u : u + 1, at:] = jnp.zeros((1, D_OUT - at), F32)
    for r in range(4):
        u = me_ref[0] ^ r
        ref = shard_refs[r]
        rows = jnp.concatenate([dw_acc[3 * u + i][:, :D_IN] for i in range(3)], axis=0)
        ref[:144, :] = jnp.concatenate([rows[:144], rows[144:]], axis=1).astype(BF)
        ref[144:, :] = jnp.where(
            iota((16, D_OUT), 0) == 0, shard_ref[pl.ds(u, 1), :], 0.0
        ).astype(BF)


def gather(me, dq, dw, pooled, wt, wpt, gain, shift, after=()):
    clips = len(pooled)
    return call(
        functools.partial(gather_body, clips),
        (1,),
        [
            (pl.BlockSpec(memory_space=pltpu.SMEM), me),
            *(whole(v) for v in (*dq, *dw, *pooled, wt, wpt, gain, shift)),
        ],
        [out_whole((160, D_OUT), BF)] * 4,
        [
            pltpu.VMEM((3 * HEADS, HEAD_DIM, EXT), F32),
            pltpu.VMEM((8, D_OUT), F32),
            pltpu.VMEM((8, D_OUT), F32),
        ],
        name="gather",
        after=after,
        cost=6,
    )


def final_body(terms, tok_ref, hg_ref, wp_ref, qkv_ref, gain_ref, dq1_ref, dq2_ref, *refs):
    part_refs, out_ref = refs[:terms], refs[-1]
    slots, _, units = tok_ref.shape[1:]
    gain = column(gain_ref)
    dq = ((dq1_ref[...] + dq2_ref[...]) * SCALE).reshape(D_OUT, 4 * units).astype(BF)
    spread = mm(wp_ref[...], hg_ref[0], 1, 1) + mm(qkv_ref[:, :D_OUT], dq, 1, 0)
    spread = spread * 0.25
    places = [slice(units * s, units * (s + 1)) for s in range(slots)]
    spread = [spread[:, places[2 * (s >> 3) + ((s >> 1) & 1)]] for s in range(slots)]
    grad = total_of(part_refs) + jnp.concatenate(spread, axis=1)
    x = jnp.concatenate([tok_ref[0, s].astype(F32) for s in range(slots)], axis=1)
    center = x - jnp.mean(x, axis=0, keepdims=True)
    inv_std = lax.rsqrt(jnp.mean(center * center, axis=0, keepdims=True) + 1e-06)
    n = center * inv_std
    e = grad * gain
    back = e - jnp.mean(e, axis=0, keepdims=True) - n * jnp.mean(e * n, axis=0, keepdims=True)
    back = back * inv_std
    for s in range(slots):
        out_ref[0, s] = back[:, places[s]]


def final(clip, tokens, hg, dq, wp, qkv, gain, parts, filled, after=()):
    terms = len(parts)
    return call(
        functools.partial(final_body, terms),
        (1,),
        [
            at_clip(tokens, clip),
            at_clip(hg, clip),
            *(whole(v) for v in (wp, qkv, gain, *dq, *parts)),
            *([] if filled is None else [(pl.BlockSpec(memory_space=pl.ANY), filled)]),
        ],
        [(at_clip(tokens, clip)[0], tokens.shape, F32)],
        name="final",
        cost=6,
        after=after,
        aliases=None if filled is None else {7 + terms: 0},
    )[0]


def unpack_first_body(
    place_ref,
    value_ref,
    other_ref,
    proj_ref,
    bproj_ref,
    wo_ref,
    bout_ref,
    gain_ref,
    shift_ref,
    we_ref,
    be_ref,
    ws_ref,
    bs_ref,
    rows_ref,
):
    half = value_ref.shape[0]
    at = pl.multiple_of(place_ref[0] * half, 8)
    rows_ref[pl.ds(at, half), :] = value_ref[...].astype(F32)
    rows_ref[pl.ds(pl.multiple_of(half - at, 8), half), :] = other_ref[...].astype(F32)
    we_ref[...] = rows_ref[:384]
    ws_ref[...] = rows_ref[384:768].T
    wo_ref[...] = rows_ref[768:864].T
    proj = jnp.concatenate([rows_ref[864:912, :D_IN], rows_ref[864:912, D_IN:]], axis=0)
    proj_ref[...] = proj.T
    lines = rows_ref[912:920]
    be_ref[...] = lines[0:1].reshape(384)
    for ref, k in ((gain_ref, 0), (shift_ref, 1), (bs_ref, 2), (bout_ref, 3), (bproj_ref, 3)):
        ref[...] = lines[1:2, 96 * k : 96 * (k + 1)].reshape(96)


def unpack_first(place, value, other, after=()):
    shapes = [(192, 96), (96,), (384, 96), (96,), (96,), (96,), (384, 384), (384,), (384, 384), (96,)]
    return call(
        unpack_first_body,
        (1,),
        [(pl.BlockSpec(memory_space=pltpu.SMEM), place), whole(value), whole(other)],
        [out_whole(shape, F32) for shape in shapes],
        [pltpu.VMEM((2 * value.shape[0], D_OUT), F32)],
        name="unpack_first",
        after=after,
        cost=2,
    )


def unpack_second_body(a_ref, b_ref, qkv_ref, bq_ref, bv_ref, gain_ref, shift_ref):
    total = a_ref[...].astype(F32) + b_ref[...].astype(F32)
    qkv_ref[...] = jnp.concatenate([total[:144, :D_IN], total[:144, D_IN:]], axis=0).T
    at = 0
    for ref in (bq_ref, bv_ref, gain_ref, shift_ref):
        size = ref.shape[0]
        ref[...] = total[144:145, at : at + size].reshape(size)
        at += size


def unpack_second(a, b):
    shapes = [(192, 288), (96,), (96,), (48,), (48,)]
    return call(
        unpack_second_body,
        (1,),
        [whole(a), whole(b)],
        [out_whole(shape, F32) for shape in shapes],
        name="unpack_second",
        cost=1,
    )


def swap_unit(value, bit):
    return lax.ppermute(value, "unit", [(i, i ^ bit) for i in range(4)])


def swap_clip(value, bit):
    size = lax.axis_size("clip")
    return lax.ppermute(value, "clip", [(i, i ^ bit) for i in range(size)])


def add(*values):
    return functools.reduce(lambda a, b: a + b, [v.astype(F32) for v in values]).astype(BF)


def member():
    at = lax.axis_index("clip").astype(jnp.int32)
    return jnp.stack([at & 1, (at >> 1) & 3])


def total_of(refs):
    return functools.reduce(lambda a, b: a + b, [ref[...].astype(F32) for ref in refs])


def between(kind, sums, place, grads=None):
    rows, width = sums[0].shape
    count, more = len(sums), grads or []
    pieces = {"plain": 1, "halves": 2, "quarters": 4, "join": 1}[kind]
    tall = rows * 4 if kind == "join" else rows // pieces

    def body(place_ref, *refs):
        terms, refs = refs[:count], refs[count:]
        others, refs = refs[: len(more)], refs[len(more) :]
        outs, scratch = refs[:-1], refs[-1]
        if more:
            outs[-1][...] = total_of(others).astype(BF)
        if kind == "plain":
            outs[0][...] = total_of(terms).astype(BF)
        elif kind == "join":
            for d in range(4):
                at = pl.multiple_of((place_ref[1] ^ d) * rows, 8)
                scratch[pl.ds(at, rows), :] = terms[d][...].astype(F32)
            outs[0][...] = scratch[...].astype(BF)
        else:
            scratch[...] = total_of(terms)
            own = place_ref[0] if kind == "halves" else place_ref[1]
            for d in range(pieces):
                at = pl.multiple_of((own ^ d) * tall, 8)
                outs[d][...] = scratch[pl.ds(at, tall), :].astype(BF)

    return call(
        body,
        (1,),
        [(pl.BlockSpec(memory_space=pltpu.SMEM), place), *(whole(v) for v in (*sums, *more))],
        [
            *([out_whole((tall, width), BF)] * pieces),
            *([out_whole(more[0].shape, BF)] if more else []),
        ],
        [pltpu.VMEM((max(rows, tall), width), F32)],
        name="between",
        cost=2,
    )


def together(*values):
    return lax.optimization_barrier(values)


def shards(
    tokens,
    first_gain,
    first_shift,
    proj_weight,
    proj_bias,
    qkv_weight,
    query_bias,
    value_bias,
    output_weight,
    output_bias,
    second_gain,
    second_shift,
    expand_weight,
    expand_bias,
    shrink_weight,
    shrink_bias,
    frame_counts,
    unit_frames,
    cotangent,
):
    clips, units = tokens.shape[:2]
    me = lax.axis_index("unit").astype(jnp.int32).reshape(1)
    vectors = [proj_bias, output_bias, second_gain, second_shift, shrink_bias, expand_bias]
    flat = tokens.transpose(0, 2, 3, 1)
    upstream = cotangent.transpose(0, 2, 1, 3).reshape(clips, 4 * units, D_OUT)
    near, across, pooled = [], [], []
    for c in range(clips):
        n, pool = normed_tokens(
            c, flat, unit_frames, frame_counts, first_gain, first_shift
        )
        near.append((n, swap_unit(n, 1)))
        pooled.append(pool)
    wt, wg, query = queries_of(qkv_weight, proj_weight, query_bias, value_bias, pooled)
    own, rest, far = [], [], []
    for c in range(clips):
        across.append(swap_unit(together(near[c][0], wt)[0] if c else near[c][0], 2))
        own.append(forward(*near[c], wt, query[c][0], after=[v[3] for v in own[-1:]]))
    for c in range(clips):
        held, _ = together(across[c], own[c][3])
        far.append((held, swap_unit(held, 1)))
        rest.append(forward(*far[c], wt, query[c][0], after=[v[3] for v in (own + rest)[-1:]]))
    out, hg, attended, factors, keep, send0, across, send1, wpt = middle(
        me,
        [value[3] for value in own],
        [value[3] for value in rest],
        pooled,
        upstream,
        vectors,
        [proj_weight, output_weight, expand_weight, shrink_weight],
    )
    dq, dw = [[None, None] for _ in range(clips)], [[None, None] for _ in range(clips)]
    place = member()
    spread = (2, 4, 6)
    got = [swap_unit(send0, 1), swap_unit(send1, 1)]
    grads = attended_grads(hg, attended, factors, output_weight)
    got, grads = together(got, grads)
    do1, do2, do1t, do2t = grads
    (value,) = between("plain", [across, got[1]], place)
    terms = [keep, got[0]]
    calls = [(c, 1) for c in range(clips)] + [(c, 0) for c in range(clips)]
    parts = [[None] * 3 for _ in range(clips)]
    lent, owed = [], []
    moves = ["unit", "halves", "quarters", "join"]
    bits = []
    bit = 8
    while bit < lax.axis_size("clip"):
        bits.append(bit)
        bit *= 2
    held = [value]
    for at, (c, side) in enumerate(calls):
        keys, kept, grads = (far, rest, (do2, do2t)) if side else (near, own, (do1, do1t))
        move = moves[at] if at < len(moves) else None
        if move == "unit":
            sent = [swap_unit(value, 2)]
        elif move == "halves":
            sent = [swap_clip(value[1], 1)]
        elif move == "quarters":
            sent = [swap_clip(v, d) for v, d in zip(value[1:], spread, strict=True)]
        elif move == "join":
            sent = [swap_clip(value, d) for d in spread]
        else:
            sent = []
        travel = [swap_unit(parts[b][0], 2) for b in lent]
        travel += [swap_unit(gb, 1) for _, gb in owed]
        result = backward(c, *keys[c], wg, *kept[c][:3], *grads, query[c][1], after=held)
        *result, travel, sent = together(*result, travel, sent)
        dq[c][side], dw[c][side], ga, gb = result
        for b in lent:
            parts[b][0] = travel.pop(0)
        lent, loose = [], None
        for ((b, other), _), arrived in zip(owed, travel, strict=True):
            if other:
                loose = [parts[b][0], arrived]
                lent.append(b)
            else:
                parts[b][2] = arrived
        if move == "unit":
            value = list(between("halves", [*terms, *sent], place, loose))
        elif move == "halves":
            value = list(between("quarters", [value[0], *sent], place, loose))
        elif move == "quarters":
            value = list(between("plain", [value[0], *sent], place, loose))
        elif move == "join":
            value = list(between("join", [value, *sent], place, loose))
        if loose and move:
            *value, parts[lent[0]][0] = value
        elif loose:
            parts[lent[0]][0] = add(*loose)
        if move in ("quarters", "join"):
            (value,) = value
        if move == "quarters":
            for bit in bits:
                value = add(value, swap_clip(value, bit))
        owed = [((c, side), gb)]
        parts[c][0 if side else 1] = ga
        held = [dq[c][side], *(value if isinstance(value, list) else [value])]
        held += [parts[b][0] for b in lent]
    other = swap_clip(value, 1)
    travel = [swap_unit(gb, 1) for _, gb in owed]
    result = gather(
        me,
        [v for pair in dq for v in pair],
        [v for pair in dw for v in pair],
        pooled,
        wt,
        wpt,
        first_gain,
        first_shift,
        after=held,
    )
    (keep, send0, across, send1), travel = together(result, travel)
    for ((b, _), _), arrived in zip(owed, travel, strict=True):
        parts[b][2] = arrived
    got = [swap_unit(send0, 1), swap_unit(send1, 1)]
    second = add(across, got[1])
    input_grad, firsts = None, None
    bit = 0
    for c in range(max(clips, 3)):
        sent = swap_clip(second, bit) if bit else swap_unit(second, 2)
        if c < clips:
            input_grad = final(
                c, flat, hg, dq[c], proj_weight, qkv_weight, first_gain, parts[c], input_grad, after=[second]
            )
            sent, input_grad = together(sent, input_grad)
        elif firsts is None:
            firsts = unpack_first(place, value, other, after=[second])
            sent, firsts = together(sent, firsts)
        if c < 3:
            second = add(second, sent) if bit else add(keep, got[0], sent)
            bit = 2 * bit if bit else 1
    if firsts is None:
        firsts = unpack_first(place, value, other)
    for more in bits:
        second = add(second, swap_clip(second, more))
    wp_grad, bp_grad, wo_grad, bo_grad, g2_grad, s2_grad, we_grad, be_grad, ws_grad, bs_grad = firsts
    qkv_grad, bq_grad, bv_grad, g1_grad, s1_grad = unpack_second(second, swap_clip(second, bit))
    return (
        out.reshape(clips, 4, units, D_OUT).transpose(0, 2, 1, 3),
        input_grad.transpose(0, 3, 1, 2),
        g1_grad,
        s1_grad,
        wp_grad,
        bp_grad,
        qkv_grad,
        bq_grad,
        bv_grad,
        wo_grad,
        bo_grad,
        g2_grad,
        s2_grad,
        we_grad,
        be_grad,
        ws_grad,
        bs_grad,
    )


def solution(mesh):
    every = P()
    split = P("clip", "unit", None, None)
    return jax.shard_map(
        shards,
        mesh=mesh,
        in_specs=(split,) + (every,) * 15 + (P("clip"), P("clip", "unit"), split),
        out_specs=(
            split,
            split,
            P("unit"),
            P("unit"),
            P(None, "unit"),
            P("unit"),
            P(None, "unit"),
            P("unit"),
            P("unit"),
            P(None, "unit"),
            P("unit"),
            P("unit"),
            P("unit"),
            P(None, "unit"),
            P("unit"),
            P("unit", None),
            P("unit"),
        ),
        check_vma=False,
    )
```

time: 284 us -> 234 us (0.82)
  waiting for transfers between devices: 31.7 us -> 4.42 us
  local copies, waits for them, and re-layouts: 18.4 us -> 6.48 us
  Pallas kernels: 194 us -> 185 us
    ppermute x16 -> x18, waiting for transfers between devices: 22.1 us -> 1.47 us  [swap_unit(): return lax.ppermute(value, 'unit', [(i, i ^ bit) for i in range(4)])]
    pallas_call x14 -> x23, Pallas kernels: 194 us -> 185 us  [call(): pl.pallas_call(run, grid=grid, in_specs=[spec for spec, _ in ins], out_sp...]
    unnamed x71 -> x6, local copies, waits for them, and re-layouts: 9.92 us -> 2.13 us
    ppermute x11, waiting for transfers between devices: 9.63 us -> 2.95 us  [swap_clip(): return lax.ppermute(value, 'clip', [(i, i ^ bit) for i in range(size)])]
    convert_element_type x15 -> x4, other arithmetic: 6.97 us -> 5.94 us  [add(): functools.reduce(lambda a, b: a + b, [v.astype(F32) for v in values])]
    ppermute x16 -> x18, starting transfers between devices: 10.9 us -> 11 us  [swap_unit(): return lax.ppermute(value, 'unit', [(i, i ^ bit) for i in range(4)])]
  transfers between devices with their start and end apart: 27 -> 29, of which waited for: 9 -> 4; matrix products, arithmetic and copies ran while one was open for 4% -> 5% of each run, Pallas kernels for 52% -> 61%
where the time goes in v2:
time: 234 us; the launch traced here: 229 us
  Pallas kernels  185 us (79%)
  starting transfers between devices  26.3 us (11%)
  other arithmetic  6.53 us (3%)
  local copies, waits for them, and re-layouts  6.48 us (3%)
  waiting for transfers between devices  4.42 us (2%)
    pallas_call x23, Pallas kernels, call(): pl.pallas_call(run, grid=grid, in_specs=[spec for spec, _ in ins], out_sp...  185 us
    ppermute x11, starting transfers between devices, swap_clip(): return lax.ppermute(value, 'clip', [(i, i ^ bit) for i in range(size)])  15.3 us
    ppermute x18, starting transfers between devices, swap_unit(): return lax.ppermute(value, 'unit', [(i, i ^ bit) for i in range(4)])  11 us
    convert_element_type x4, other arithmetic, add(): functools.reduce(lambda a, b: a + b, [v.astype(F32) for v in values])  5.94 us
  transfers between devices with their start and end apart: 29, of which 4 were waited for; matrix products, arithmetic and copies ran while one was open for 5% of the time, Pallas kernels for 61%

profile of v2, /device:TPU:0, one launch (start us, length us, event | category | flops | bytes accessed | tf_op | source)
XLA Modules:
  0.0 229.3 jit_solution(15647970800473801191)
XLA Ops:
  0.7 3.0 %normed.2 = (bf16[208,1568]{1,0:T(8,128)(2,1)}, bf16[392,256]{1,0:T(8,128)(2,1)}) custom-call(bf16[2,16,192,98]{3,2,1,0:T(8,128)(2,1)} %bitcast.13, s32[2,98]{1,0:T(2,128)} %refs_1_.4, s32[2]{0:T(128)} %refs_2_.6, bf16[192]{0:T(256)(128)(2,1)} %refs_4_.7, bf16[192]{0:T(256)(128)(2,1)} %refs_14_.3), custom_call_target="tpu_custom_call" | custom-call | flops 3300000000 | bytes 3000000 | tf_op jit(solution)/shard_map/normed/pallas_call | solution.py:40
  3.7 2.9 %collective-permute-start.2 = (bf16[208,1568]{1,0:T(8,128)(2,1)}, bf16[208,1568]{1,0:T(8,128)(2,1)}, u32[]{:S(2)}, u32[]{:S(2)}) collective-permute-start(bf16[208,1568]{1,0:T(8,128)(2,1)} %get-tuple-element.158.refs_0_), channel_id=1, source_target_pairs={{0,2},{1,3},{2,0},{3,1},{4,6},{5,7},{6,4},{7,5},{8,10},{9,11},{10,... | collective-permute-start | bytes 1956872 | tf_op jit(solution)/shard_map/ppermute | solution.py:682
  6.6 3.0 %normed.3 = (bf16[208,1568]{1,0:T(8,128)(2,1)}, bf16[392,256]{1,0:T(8,128)(2,1)}) custom-call(bf16[2,16,192,98]{3,2,1,0:T(8,128)(2,1)} %bitcast.14, s32[2,98]{1,0:T(2,128)} %refs_1_.4, s32[2]{0:T(128)} %refs_2_.6, bf16[192]{0:T(256)(128)(2,1)} %refs_4_.7, bf16[192]{0:T(256)(128)(2,1)} %refs_14_.3), custom_call_target="tpu_custom_call" | custom-call | flops 3300000000 | bytes 3000000 | tf_op jit(solution)/shard_map/normed/pallas_call | solution.py:40
  10.1 4.1 %queries.1 = (bf16[15,128,256]{2,1,0:T(8,128)(2,1)}, bf16[192,768]{1,0:T(8,128)(2,1)}, bf16[4,392,128]{2,1,0:T(8,128)(2,1)}, bf16[4,96,392]{2,1,0:T(8,128)(2,1)}...) custom-call(bf16[192,1152]{1,0:T(8,128)(2,1)} %refs_3_.11, bf16[192,384]{1,0:T(8,128)(2,1)} %refs_2_.9, ...), custom_call_target="tpu_custom_call" | custom-call | flops 5500000256 | bytes 5000000 | tf_op jit(solution)/shard_map/queries/pallas_call | solution.py:40
  16.7 13.5 %attend.4 = (bf16[4,392,3136]{2,1,0:T(8,128)(2,1)}, bf16[4,128,3136]{2,1,0:T(8,128)(2,1)}, bf16[4,128,3136]{2,1,0:T(8,128)(2,1)}, f32[4,128,392]{2,1,0:T(8,128)}) custom-call(bf16[208,1568]{1,0:T(8,128)(2,1)} %get-tuple-element.158.refs_0_, bf16[208,1568]{1,0:T(8,128)(2,1)} %collective-permute-done.refs_1_, ...), custom_call_target="tpu_custom_call" | custom-call | flops 13200000000 | bytes 12000000 | tf_op jit(solution)/shard_map/attend/pallas_call | solution.py:40
  30.2 13.1 %attend.5 = (bf16[4,392,3136]{2,1,0:T(8,128)(2,1)}, bf16[4,128,3136]{2,1,0:T(8,128)(2,1)}, bf16[4,128,3136]{2,1,0:T(8,128)(2,1)}, f32[4,128,392]{2,1,0:T(8,128)}) custom-call(bf16[208,1568]{1,0:T(8,128)(2,1)} %get-tuple-element.169.refs_0_, bf16[208,1568]{1,0:T(8,128)(2,1)} %collective-permute-done.1.refs_1_, ...), custom_call_target="tpu_custom_call" | custom-call | flops 13200000000 | bytes 12000000 | tf_op jit(solution)/shard_map/attend/pallas_call | solution.py:40
  43.9 13.0 %attend.6 = (bf16[4,392,3136]{2,1,0:T(8,128)(2,1)}, bf16[4,128,3136]{2,1,0:T(8,128)(2,1)}, bf16[4,128,3136]{2,1,0:T(8,128)(2,1)}, f32[4,128,392]{2,1,0:T(8,128)}) custom-call(bf16[208,1568]{1,0:T(8,128)(2,1)} %collective-permute-done.2.refs_0_, bf16[208,1568]{1,0:T(8,128)(2,1)} %collective-permute-done.3.refs_1_, ...), custom_call_target="tpu_custom_call" | custom-call | flops 13200000000 | bytes 12000000 | tf_op jit(solution)/shard_map/attend/pallas_call | solution.py:40
  56.9 13.3 %attend.7 = (bf16[4,392,3136]{2,1,0:T(8,128)(2,1)}, bf16[4,128,3136]{2,1,0:T(8,128)(2,1)}, bf16[4,128,3136]{2,1,0:T(8,128)(2,1)}, f32[4,128,392]{2,1,0:T(8,128)}) custom-call(bf16[208,1568]{1,0:T(8,128)(2,1)} %collective-permute-done.4.refs_0_, bf16[208,1568]{1,0:T(8,128)(2,1)} %collective-permute-done.5.refs_1_, ...), custom_call_target="tpu_custom_call" | custom-call | flops 13200000000 | bytes 12000000 | tf_op jit(solution)/shard_map/attend/pallas_call | solution.py:40
  70.2 16.6 %middle.1 = (f32[2,392,384]{2,1,0:T(8,128)}, bf16[2,392,384]{2,1,0:T(8,128)(2,1)}, f32[2,4,96,392]{3,2,1,0:T(8,128)}, f32[2,4,8,392]{3,2,1,0:T(8,128)}, bf16[960...) custom-call(s32[1]{0:T(128)} %bitcast.refs_0_, ...), custom_call_target="tpu_custom_call" | custom-call | flops 17600000000 | bytes 16000000 | tf_op jit(solution)/shard_map/middle/pallas_call | solution.py:40
  88.0 4.2 %attended_grads.1 = (bf16[2,4,392,128]{3,2,1,0:T(8,128)(2,1)}, bf16[2,4,392,128]{3,2,1,0:T(8,128)(2,1)}, bf16[2,4,96,392]{3,2,1,0:T(8,128)(2,1)}, bf16[2,4,96,392]{3,2,1,0:T(8,128)(2,1)}) custom-call(bf16[2,392,384]{2,1,0:T(8,128)(2,1)} %get-tuple-element.179.refs_0_.refs_1_, f32[2,4,96,392]{3,2,1,0:T(8,128)} %get-tuple-element.180.refs_1_, ...), custom_call_target="tpu_custom_call" | custom-call | flops 5500000256 | bytes 5000000 | tf_op jit(solution)/shard_map/attended_grads/pallas_call | solution.py:40
  92.3 2.4 %between.5.refs_9_ = bf16[960,384]{1,0:T(8,128)(2,1)} custom-call(s32[2]{0:T(128)} %pad_add_fusion.refs_0_, bf16[960,384]{1,0:T(8,128)(2,1)} %get-tuple-element.198.refs_1_, bf16[960,384]{1,0:T(8,128)(2,1)} %collective-permute-done.7.refs_2_), custom_call_target="tpu_custom_call" | custom-call | flops 2200000000 | bytes 2000000 | tf_op jit(solution)/shard_map/between/pallas_call | solution.py:40
  94.7 2.1 collective-permute-start.8
  96.8 16.6 %attend_back.4 = (f32[4,96,392]{2,1,0:T(8,128)}, f32[768,208]{1,0:T(8,128)}, bf16[192,1568]{1,0:T(8,128)(2,1)}, bf16[192,1568]{1,0:T(8,128)(2,1)}) custom-call(bf16[208,1568]{1,0:T(8,128)(2,1)} %collective-permute-done.2.refs_0_, bf16[208,1568]{1,0:T(8,128)(2,1)} %collective-permute-done.3.refs_1_, bf16[192,768]{1,0:T(8,128)(2,1)} %get-tuple-element.173.refs_2_, ...), custom_call_target="tpu_custom_call" | custom-call | flops 18699999232 | bytes 17000000 | tf_op jit(solution)/shard_map/attend_back/pallas_call | solution.py:40
  113.8 2.9 %between.6 = (bf16[480,384]{1,0:T(8,128)(2,1)}, bf16[480,384]{1,0:T(8,128)(2,1)}) custom-call(s32[2]{0:T(128)} %pad_add_fusion.refs_0_, bf16[960,384]{1,0:T(8,128)(2,1)} %get-tuple-element.205.refs_1_, bf16[960,384]{1,0:T(8,128)(2,1)} %collective-permute-done.6.refs_2_, bf16[960,384]{1,0:T(8,128)(2,1)} %collective-permute-done.8.refs_3_), custom_call_target="tpu_custom_call" | custom-call | flops 2200000000 | bytes 2000000 | tf_op jit(solution)/shard_map/between/pallas_call | solution.py:40
  116.7 1.8 collective-permute-start.10
  118.5 16.5 %attend_back.5 = (f32[4,96,392]{2,1,0:T(8,128)}, f32[768,208]{1,0:T(8,128)}, bf16[192,1568]{1,0:T(8,128)(2,1)}, bf16[192,1568]{1,0:T(8,128)(2,1)}) custom-call(bf16[208,1568]{1,0:T(8,128)(2,1)} %collective-permute-done.4.refs_0_, bf16[208,1568]{1,0:T(8,128)(2,1)} %collective-permute-done.5.refs_1_, bf16[192,768]{1,0:T(8,128)(2,1)} %get-tuple-element.173.refs_2_, ...), custom_call_target="tpu_custom_call" | custom-call | flops 18699999232 | bytes 17000000 | tf_op jit(solution)/shard_map/attend_back/pallas_call | solution.py:40
  135.0 2.8 %between.7 = (bf16[120,384]{1,0:T(8,128)(2,1)}, bf16[120,384]{1,0:T(8,128)(2,1)}, bf16[120,384]{1,0:T(8,128)(2,1)}, bf16[120,384]{1,0:T(8,128)(2,1)}, bf16[192,1568]{1,0:T(8,128)(2,1)}) custom-call(s32[2]{0:T(128)} %pad_add_fusion.refs_0_, bf16[480,384]{1,0:T(8,128)(2,1)} %get-tuple-element.208.refs_10_.refs_1_, ...), custom_call_target="tpu_custom_call" | custom-call | flops 2200000000 | bytes 2000000 | tf_op jit(solution)/shard_map/between/pallas_call | solution.py:40
  139.4 2.6 %collective-permute-start.14 = (bf16[120,384]{1,0:T(8,128)(2,1)}, bf16[120,384]{1,0:T(8,128)(2,1)}, u32[]{:S(2)}, u32[]{:S(2)}) collective-permute-start(bf16[120,384]{1,0:T(8,128)(2,1)} %get-tuple-element.221.refs_12_), channel_id=1, source_target_pairs={{0,16},{4,20},{8,24},{12,28},{16,0},{20,4},{24,8},{28,12},{1,17},{... | collective-permute-start | bytes 276488 | tf_op jit(solution)/shard_map/ppermute | solution.py:687
  143.7 16.8 %attend_back.6 = (f32[4,96,392]{2,1,0:T(8,128)}, f32[768,208]{1,0:T(8,128)}, bf16[192,1568]{1,0:T(8,128)(2,1)}, bf16[192,1568]{1,0:T(8,128)(2,1)}) custom-call(bf16[208,1568]{1,0:T(8,128)(2,1)} %get-tuple-element.158.refs_0_, bf16[208,1568]{1,0:T(8,128)(2,1)} %collective-permute-done.refs_1_, bf16[192,768]{1,0:T(8,128)(2,1)} %get-tuple-element.173.refs_2_, ...), custom_call_target="tpu_custom_call" | custom-call | flops 18699999232 | bytes 17000000 | tf_op jit(solution)/shard_map/attend_back/pallas_call | solution.py:40
  160.5 2.5 %between.8 = (bf16[120,384]{1,0:T(8,128)(2,1)}, bf16[192,1568]{1,0:T(8,128)(2,1)}) custom-call(s32[2]{0:T(128)} %pad_add_fusion.refs_0_, bf16[120,384]{1,0:T(8,128)(2,1)} %get-tuple-element.219.refs_10_.refs_1_, bf16[120,384]{1,0:T(8,128)(2,1)} %collective-permute-done.13.refs_2_, bf16[120,384]{1,0:T(8,128)(2,1)} %collective-permute-done.14.refs_3_, ...), custom_call_target="tpu_custom_call" | custom-call | flops 2200000000 | bytes 2000000 | tf_op jit(solution)/shard_map/between/pallas_call | solution.py:40
  163.0 3.6 %collective-permute-start.20 = (bf16[120,384]{1,0:T(8,128)(2,1)}, bf16[120,384]{1,0:T(8,128)(2,1)}, u32[]{:S(2)}, u32[]{:S(2)}) collective-permute-start(bf16[120,384]{1,0:T(8,128)(2,1)} %get-tuple-element.238.refs_10_.refs_1_), channel_id=1, source_target_pairs={{0,24},{4,28},{8,16},{12,20},{16,8},{20,12},{24,0},{28,4},{1,25},{... | collective-permute-start | bytes 276488 | tf_op jit(solution)/shard_map/ppermute | solution.py:687
  167.9 16.6 %attend_back.7 = (f32[4,96,392]{2,1,0:T(8,128)}, f32[768,208]{1,0:T(8,128)}, bf16[192,1568]{1,0:T(8,128)(2,1)}, bf16[192,1568]{1,0:T(8,128)(2,1)}) custom-call(bf16[208,1568]{1,0:T(8,128)(2,1)} %get-tuple-element.169.refs_0_, bf16[208,1568]{1,0:T(8,128)(2,1)} %collective-permute-done.1.refs_1_, bf16[192,768]{1,0:T(8,128)(2,1)} %get-tuple-element.173.refs_2_, ...), custom_call_target="tpu_custom_call" | custom-call | flops 18699999232 | bytes 17000000 | tf_op jit(solution)/shard_map/attend_back/pallas_call | solution.py:40
  185.1 1.9 between.9.refs_16_.refs_1_
  187.0 5.3 %gather.1 = (bf16[160,384]{1,0:T(8,128)(2,1)}, bf16[160,384]{1,0:T(8,128)(2,1)}, bf16[160,384]{1,0:T(8,128)(2,1)}, bf16[160,384]{1,0:T(8,128)(2,1)}) custom-call(s32[1]{0:T(128)} %bitcast.refs_0_, f32[4,96,392]{2,1,0:T(8,128)} %get-tuple-element.229.refs_9_.refs_1_.refs_5_, f32[4,96,392]{2,1,0:T(8,128)} %get-tuple-element.204.refs_9_.refs_2_.refs_6_, ...), custom_call_target="tpu_custom_call" | custom-call | flops 6600000000 | bytes 6000000 | tf_op jit(solution)/shard_map/gather/pallas_call | solution.py:40
  197.0 5.9 %final.2.refs_10_ = f32[2,16,192,98]{3,2,1,0:T(8,128)} custom-call(bf16[2,16,192,98]{3,2,1,0:T(8,128)(2,1)} %bitcast.15, bf16[2,392,384]{2,1,0:T(8,128)(2,1)} %get-tuple-element.179.refs_0_.refs_1_, bf16[192,384]{1,0:T(8,128)(2,1)} %refs_2_.9, bf16[192,1152]{1,0:T(8,128)(2,1)} %refs_3_.11, bf16[192]{0:T(256)(128)(2,1)} %refs_4_.7, ...), custom_call_target="tpu_custom_call" | custom-call | flops 6600000000 | bytes 6000000 | tf_op jit(solution)/shard_map/final/pallas_call | solution.py:40
  202.9 1.7 add_convert_fusion.2.refs_11_
  205.4 5.9 %final.3 = f32[2,16,192,98]{3,2,1,0:T(8,128)} custom-call(bf16[2,16,192,98]{3,2,1,0:T(8,128)(2,1)} %bitcast.16, bf16[2,392,384]{2,1,0:T(8,128)(2,1)} %get-tuple-element.179.refs_0_.refs_1_, bf16[192,384]{1,0:T(8,128)(2,1)} %refs_2_.9, bf16[192,1152]{1,0:T(8,128)(2,1)} %refs_3_.11, bf16[192]{0:T(256)(128)(2,1)} %refs_4_.7, ...), custom_call_target="tpu_custom_call", output_to_operand_aliasing={{}: (10, {})} | custom-call | flops 6600000000 | bytes 6000000 | tf_op jit(solution)/shard_map/final/pallas_call | solution.py:40
  211.3 1.6 add_convert_fusion.1.refs_3_
  214.2 2.6 %unpack_first.1 = (f32[192,96]{1,0:T(8,128)}, f32[96]{0:T(128)}, f32[384,96]{1,0:T(8,128)}, f32[96]{0:T(128)}, f32[96]{0:T(128)}, /*index=5*/f32[96]{0:T(128)}, ...) custom-call(s32[2]{0:T(128)} %pad_add_fusion.refs_0_, bf16[480,384]{1,0:T(8,128)(2,1)} %between.9.refs_16_.refs_1_, ...), custom_call_target="tpu_custom_call" | custom-call | flops 2200000000 | bytes 2000000 | tf_op jit(solution)/shard_map/unpack_first/pallas_call | solution.py:40
  219.3 2.5 %collective-permute-start.28 = (bf16[160,384]{1,0:T(8,128)(2,1)S(1)}, bf16[160,384]{1,0:T(8,128)(2,1)}, u32[]{:S(2)}, u32[]{:S(2)}) collective-permute-start(bf16[160,384]{1,0:T(8,128)(2,1)S(1)} %add_convert_fusion.refs_0_), channel_id=1, source_target_pairs={{0,16},{4,20},{8,24},{12,28},{16,0},{20,4},{24,8},{28,12},{1,17},{... | collective-permute-start | bytes 368648 | tf_op jit(solution)/shard_map/ppermute | solution.py:687
  221.8 1.9 copy.42
  227.2 1.9 unpack_second.1
  (63 shorter events, 23.0 us)
Async XLA Ops:
  3.7 26.5 %collective-permute-start.2 = (bf16[208,1568]{1,0:T(8,128)(2,1)}, bf16[208,1568]{1,0:T(8,128)(2,1)}, u32[]{:S(2)}, u32[]{:S(2)}) collective-permute-start(bf16[208,1568]{1,0:T(8,128)(2,1)} %get-tuple-element.158.refs_0_), channel_id=1, source_target_pairs={{0,2},{1,3},{2,0},{3,1},{4,6},{5,7},{6,4},{7,5},{8,10},{9,11},{10,... | collective-permute-start | bytes 1956872 | tf_op jit(solution)/shard_map/ppermute | solution.py:682
  6.6 10.0 %collective-permute-start = (bf16[208,1568]{1,0:T(8,128)(2,1)}, bf16[208,1568]{1,0:T(8,128)(2,1)}, u32[]{:S(2)}, u32[]{:S(2)}) collective-permute-start(bf16[208,1568]{1,0:T(8,128)(2,1)} %get-tuple-element.158.refs_0_), channel_id=1, source_target_pairs={{0,1},{1,0},{2,3},{3,2},{4,5},{5,4},{6,7},{7,6},{8,9},{9,8},{10,11... | collective-permute-start | bytes 1956872 | tf_op jit(solution)/shard_map/ppermute | solution.py:682
  9.6 20.6 %collective-permute-start.1 = (bf16[208,1568]{1,0:T(8,128)(2,1)}, bf16[208,1568]{1,0:T(8,128)(2,1)}, u32[]{:S(2)}, u32[]{:S(2)}) collective-permute-start(bf16[208,1568]{1,0:T(8,128)(2,1)} %get-tuple-element.169.refs_0_), channel_id=1, source_target_pairs={{0,1},{1,0},{2,3},{3,2},{4,5},{5,4},{6,7},{7,6},{8,9},{9,8},{10,11... | collective-permute-start | bytes 1956872 | tf_op jit(solution)/shard_map/ppermute | solution.py:682
  14.2 29.1 %collective-permute-start.4 = (bf16[208,1568]{1,0:T(8,128)(2,1)}, bf16[208,1568]{1,0:T(8,128)(2,1)}, u32[]{:S(2)}, u32[]{:S(2)}) collective-permute-start(bf16[208,1568]{1,0:T(8,128)(2,1)} %get-tuple-element.169.refs_0_), channel_id=1, source_target_pairs={{0,2},{1,3},{2,0},{3,1},{4,6},{5,7},{6,4},{7,5},{8,10},{9,11},{10,... | collective-permute-start | bytes 1956872 | tf_op jit(solution)/shard_map/ppermute | solution.py:682
  30.1 13.7 %collective-permute-start.3 = (bf16[208,1568]{1,0:T(8,128)(2,1)}, bf16[208,1568]{1,0:T(8,128)(2,1)}, u32[]{:S(2)}, u32[]{:S(2)}) collective-permute-start(bf16[208,1568]{1,0:T(8,128)(2,1)} %collective-permute-done.2.refs_0_), channel_id=1, source_target_pairs={{0,1},{1,0},{2,3},{3,2},{4,5},{5,4},{6,7},{7,6},{8,9},{9,8},{10,11... | collective-permute-start | bytes 1956872 | tf_op jit(solution)/shard_map/ppermute | solution.py:682
  43.3 13.6 %collective-permute-start.5 = (bf16[208,1568]{1,0:T(8,128)(2,1)}, bf16[208,1568]{1,0:T(8,128)(2,1)}, u32[]{:S(2)}, u32[]{:S(2)}) collective-permute-start(bf16[208,1568]{1,0:T(8,128)(2,1)} %collective-permute-done.4.refs_0_), channel_id=1, source_target_pairs={{0,1},{1,0},{2,3},{3,2},{4,5},{5,4},{6,7},{7,6},{8,9},{9,8},{10,11... | collective-permute-start | bytes 1956872 | tf_op jit(solution)/shard_map/ppermute | solution.py:682
  86.9 5.4 %collective-permute-start.6 = (bf16[960,384]{1,0:T(8,128)(2,1)}, bf16[960,384]{1,0:T(8,128)(2,1)}, u32[]{:S(2)}, u32[]{:S(2)}) collective-permute-start(bf16[960,384]{1,0:T(8,128)(2,1)} %get-tuple-element.177), channel_id=1, source_target_pairs={{0,1},{1,0},{2,3},{3,2},{4,5},{5,4},{6,7},{7,6},{8,9},{9,8},{10,11... | collective-permute-start | bytes 2211848 | tf_op jit(solution)/shard_map/ppermute | solution.py:682
  87.0 5.3 %collective-permute-start.7 = (bf16[960,384]{1,0:T(8,128)(2,1)}, bf16[960,384]{1,0:T(8,128)(2,1)}, u32[]{:S(2)}, u32[]{:S(2)}) collective-permute-start(bf16[960,384]{1,0:T(8,128)(2,1)} %get-tuple-element.178), channel_id=1, source_target_pairs={{0,1},{1,0},{2,3},{3,2},{4,5},{5,4},{6,7},{7,6},{8,9},{9,8},{10,11... | collective-permute-start | bytes 2211848 | tf_op jit(solution)/shard_map/ppermute | solution.py:682
  94.7 19.1 %collective-permute-start.8 = (bf16[960,384]{1,0:T(8,128)(2,1)}, bf16[960,384]{1,0:T(8,128)(2,1)}, u32[]{:S(2)}, u32[]{:S(2)}) collective-permute-start(bf16[960,384]{1,0:T(8,128)(2,1)} %between.5.refs_9_), channel_id=1, source_target_pairs={{0,2},{1,3},{2,0},{3,1},{4,6},{5,7},{6,4},{7,5},{8,10},{9,11},{10,... | collective-permute-start | bytes 2211848 | tf_op jit(solution)/shard_map/ppermute | solution.py:682
  116.7 18.2 %collective-permute-start.10 = (bf16[480,384]{1,0:T(8,128)(2,1)}, bf16[480,384]{1,0:T(8,128)(2,1)}, u32[]{:S(2)}, u32[]{:S(2)}) collective-permute-start(bf16[480,384]{1,0:T(8,128)(2,1)} %get-tuple-element.209.refs_11_), channel_id=1, source_target_pairs={{0,4},{4,0},{8,12},{12,8},{16,20},{20,16},{24,28},{28,24},{1,5},{5... | collective-permute-start | bytes 1105928 | tf_op jit(solution)/shard_map/ppermute | solution.py:687
  118.5 16.5 %collective-permute-start.9 = (bf16[192,1568]{1,0:T(8,128)(2,1)}, bf16[192,1568]{1,0:T(8,128)(2,1)}, u32[]{:S(2)}, u32[]{:S(2)}) collective-permute-start(bf16[192,1568]{1,0:T(8,128)(2,1)} %get-tuple-element.214), channel_id=1, source_target_pairs={{0,1},{1,0},{2,3},{3,2},{4,5},{5,4},{6,7},{7,6},{8,9},{9,8},{10,11... | collective-permute-start | bytes 1806344 | tf_op jit(solution)/shard_map/ppermute | solution.py:682
  137.8 22.7 %collective-permute-start.13 = (bf16[120,384]{1,0:T(8,128)(2,1)}, bf16[120,384]{1,0:T(8,128)(2,1)}, u32[]{:S(2)}, u32[]{:S(2)}) collective-permute-start(bf16[120,384]{1,0:T(8,128)(2,1)} %get-tuple-element.220.refs_11_), channel_id=1, source_target_pairs={{0,8},{4,12},{8,0},{12,4},{16,24},{20,28},{24,16},{28,20},{1,9},{5... | collective-permute-start | bytes 276488 | tf_op jit(solution)/shard_map/ppermute | solution.py:687
  139.4 21.1 %collective-permute-start.14 = (bf16[120,384]{1,0:T(8,128)(2,1)}, bf16[120,384]{1,0:T(8,128)(2,1)}, u32[]{:S(2)}, u32[]{:S(2)}) collective-permute-start(bf16[120,384]{1,0:T(8,128)(2,1)} %get-tuple-element.221.refs_12_), channel_id=1, source_target_pairs={{0,16},{4,20},{8,24},{12,28},{16,0},{20,4},{24,8},{28,12},{1,17},{... | collective-permute-start | bytes 276488 | tf_op jit(solution)/shard_map/ppermute | solution.py:687
  142.0 18.5 %collective-permute-start.15 = (bf16[120,384]{1,0:T(8,128)(2,1)}, bf16[120,384]{1,0:T(8,128)(2,1)}, u32[]{:S(2)}, u32[]{:S(2)}) collective-permute-start(bf16[120,384]{1,0:T(8,128)(2,1)} %get-tuple-element.222.refs_13_), channel_id=1, source_target_pairs={{0,24},{4,28},{8,16},{12,20},{16,8},{20,12},{24,0},{28,4},{1,25},{... | collective-permute-start | bytes 276488 | tf_op jit(solution)/shard_map/ppermute | solution.py:687
  142.2 18.3 %collective-permute-start.11 = (bf16[192,1568]{1,0:T(8,128)(2,1)}, bf16[192,1568]{1,0:T(8,128)(2,1)}, u32[]{:S(2)}, u32[]{:S(2)}) collective-permute-start(bf16[192,1568]{1,0:T(8,128)(2,1)} %get-tuple-element.223.refs_14_), channel_id=1, source_target_pairs={{0,2},{1,3},{2,0},{3,1},{4,6},{5,7},{6,4},{7,5},{8,10},{9,11},{10,... | collective-permute-start | bytes 1806344 | tf_op jit(solution)/shard_map/ppermute | solution.py:682
  143.7 16.8 %collective-permute-start.12 = (bf16[192,1568]{1,0:T(8,128)(2,1)}, bf16[192,1568]{1,0:T(8,128)(2,1)}, u32[]{:S(2)}, u32[]{:S(2)}) collective-permute-start(bf16[192,1568]{1,0:T(8,128)(2,1)} %get-tuple-element.228), channel_id=1, source_target_pairs={{0,1},{1,0},{2,3},{3,2},{4,5},{5,4},{6,7},{7,6},{8,9},{9,8},{10,11... | collective-permute-start | bytes 1806344 | tf_op jit(solution)/shard_map/ppermute | solution.py:682
  163.0 21.6 %collective-permute-start.20 = (bf16[120,384]{1,0:T(8,128)(2,1)}, bf16[120,384]{1,0:T(8,128)(2,1)}, u32[]{:S(2)}, u32[]{:S(2)}) collective-permute-start(bf16[120,384]{1,0:T(8,128)(2,1)} %get-tuple-element.238.refs_10_.refs_1_), channel_id=1, source_target_pairs={{0,24},{4,28},{8,16},{12,20},{16,8},{20,12},{24,0},{28,4},{1,25},{... | collective-permute-start | bytes 276488 | tf_op jit(solution)/shard_map/ppermute | solution.py:687
  166.6 18.0 %collective-permute-start.19 = (bf16[120,384]{1,0:T(8,128)(2,1)}, bf16[120,384]{1,0:T(8,128)(2,1)}, u32[]{:S(2)}, u32[]{:S(2)}) collective-permute-start(bf16[120,384]{1,0:T(8,128)(2,1)} %get-tuple-element.238.refs_10_.refs_1_), channel_id=1, source_target_pairs={{0,16},{4,20},{8,24},{12,28},{16,0},{20,4},{24,8},{28,12},{1,17},{... | collective-permute-start | bytes 276488 | tf_op jit(solution)/shard_map/ppermute | solution.py:687
  166.6 18.0 %collective-permute-start.18 = (bf16[120,384]{1,0:T(8,128)(2,1)}, bf16[120,384]{1,0:T(8,128)(2,1)}, u32[]{:S(2)}, u32[]{:S(2)}) collective-permute-start(bf16[120,384]{1,0:T(8,128)(2,1)} %get-tuple-element.238.refs_10_.refs_1_), channel_id=1, source_target_pairs={{0,8},{4,12},{8,0},{12,4},{16,24},{20,28},{24,16},{28,20},{1,9},{5... | collective-permute-start | bytes 276488 | tf_op jit(solution)/shard_map/ppermute | solution.py:687
  167.4 17.2 %collective-permute-start.16 = (bf16[192,1568]{1,0:T(8,128)(2,1)}, bf16[192,1568]{1,0:T(8,128)(2,1)}, u32[]{:S(2)}, u32[]{:S(2)}) collective-permute-start(bf16[192,1568]{1,0:T(8,128)(2,1)} %get-tuple-element.239.refs_11_), channel_id=1, source_target_pairs={{0,2},{1,3},{2,0},{3,1},{4,6},{5,7},{6,4},{7,5},{8,10},{9,11},{10,... | collective-permute-start | bytes 1806344 | tf_op jit(solution)/shard_map/ppermute | solution.py:682
  167.9 16.6 %collective-permute-start.17 = (bf16[192,1568]{1,0:T(8,128)(2,1)}, bf16[192,1568]{1,0:T(8,128)(2,1)}, u32[]{:S(2)}, u32[]{:S(2)}) collective-permute-start(bf16[192,1568]{1,0:T(8,128)(2,1)} %get-tuple-element.244), channel_id=1, source_target_pairs={{0,1},{1,0},{2,3},{3,2},{4,5},{5,4},{6,7},{7,6},{8,9},{9,8},{10,11... | collective-permute-start | bytes 1806344 | tf_op jit(solution)/shard_map/ppermute | solution.py:682
  184.6 7.7 %collective-permute-start.21 = (bf16[192,1568]{1,0:T(8,128)(2,1)}, bf16[192,1568]{1,0:T(8,128)(2,1)}, u32[]{:S(2)}, u32[]{:S(2)}) collective-permute-start(bf16[192,1568]{1,0:T(8,128)(2,1)} %get-tuple-element.258), channel_id=1, source_target_pairs={{0,1},{1,0},{2,3},{3,2},{4,5},{5,4},{6,7},{7,6},{8,9},{9,8},{10,11... | collective-permute-start | bytes 1806344 | tf_op jit(solution)/shard_map/ppermute | solution.py:682
  192.3 1.6 collective-permute-start.23
  192.4 21.8 %collective-permute-start.27 = (bf16[480,384]{1,0:T(8,128)(2,1)}, bf16[480,384]{1,0:T(8,128)(2,1)}, u32[]{:S(2)}, u32[]{:S(2)}) collective-permute-start(bf16[480,384]{1,0:T(8,128)(2,1)} %between.9.refs_16_.refs_1_), channel_id=1, source_target_pairs={{0,4},{4,0},{8,12},{12,8},{16,20},{20,16},{24,28},{28,24},{1,5},{5... | collective-permute-start | bytes 1105928 | tf_op jit(solution)/shard_map/ppermute | solution.py:687
  192.7 10.2 %collective-permute-start.22 = (bf16[160,384]{1,0:T(8,128)(2,1)}, bf16[160,384]{1,0:T(8,128)(2,1)}, u32[]{:S(2)}, u32[]{:S(2)}) collective-permute-start(bf16[160,384]{1,0:T(8,128)(2,1)} %get-tuple-element.260), channel_id=1, source_target_pairs={{0,1},{1,0},{2,3},{3,2},{4,5},{5,4},{6,7},{7,6},{8,9},{9,8},{10,11... | collective-permute-start | bytes 368648 | tf_op jit(solution)/shard_map/ppermute | solution.py:682
  195.5 7.4 %collective-permute-start.24 = (bf16[160,384]{1,0:T(8,128)(2,1)}, bf16[160,384]{1,0:T(8,128)(2,1)}, u32[]{:S(2)}, u32[]{:S(2)}) collective-permute-start(bf16[160,384]{1,0:T(8,128)(2,1)} %add_convert_fusion.3.refs_10_), channel_id=1, source_target_pairs={{0,2},{1,3},{2,0},{3,1},{4,6},{5,7},{6,4},{7,5},{8,10},{9,11},{10,... | collective-permute-start | bytes 368648 | tf_op jit(solution)/shard_map/ppermute | solution.py:682
  204.6 6.7 %collective-permute-start.25 = (bf16[160,384]{1,0:T(8,128)(2,1)}, bf16[160,384]{1,0:T(8,128)(2,1)}, u32[]{:S(2)}, u32[]{:S(2)}) collective-permute-start(bf16[160,384]{1,0:T(8,128)(2,1)} %add_convert_fusion.2.refs_11_), channel_id=1, source_target_pairs={{0,4},{4,0},{8,12},{12,8},{16,20},{20,16},{24,28},{28,24},{1,5},{5... | collective-permute-start | bytes 368648 | tf_op jit(solution)/shard_map/ppermute | solution.py:687
  212.9 5.3 %collective-permute-start.26 = (bf16[160,384]{1,0:T(8,128)(2,1)}, bf16[160,384]{1,0:T(8,128)(2,1)}, u32[]{:S(2)}, u32[]{:S(2)}) collective-permute-start(bf16[160,384]{1,0:T(8,128)(2,1)} %add_convert_fusion.1.refs_3_), channel_id=1, source_target_pairs={{0,8},{4,12},{8,0},{12,4},{16,24},{20,28},{24,16},{28,20},{1,9},{5... | collective-permute-start | bytes 368648 | tf_op jit(solution)/shard_map/ppermute | solution.py:687
  216.8 8.2 %copy-start = (f32[384,96]{1,0:T(8,128)S(1)}, f32[384,96]{1,0:T(8,128)}, u32[]{:S(2)}) copy-start(f32[384,96]{1,0:T(8,128)} %get-tuple-element.325) | copy-start | bytes 442372
  219.3 6.5 %copy-start.1 = (bf16[160,384]{1,0:T(8,128)(2,1)}, bf16[160,384]{1,0:T(8,128)(2,1)S(1)}, u32[]{:S(2)}) copy-start(bf16[160,384]{1,0:T(8,128)(2,1)S(1)} %add_convert_fusion.refs_0_) | copy-start | bytes 368644
  219.3 7.9 %collective-permute-start.28 = (bf16[160,384]{1,0:T(8,128)(2,1)S(1)}, bf16[160,384]{1,0:T(8,128)(2,1)}, u32[]{:S(2)}, u32[]{:S(2)}) collective-permute-start(bf16[160,384]{1,0:T(8,128)(2,1)S(1)} %add_convert_fusion.refs_0_), channel_id=1, source_target_pairs={{0,16},{4,20},{8,24},{12,28},{16,0},{20,4},{24,8},{28,12},{1,17},{... | collective-permute-start | bytes 368648 | tf_op jit(solution)/shard_map/ppermute | solution.py:687
